TPU v7x, 32 devices: a whole 2x2x4 slice. The times are simulated.
32 devices in a mesh: dp: 8 (over z, x), head: 4 (over y, core).
Axes of the slice: x: 2, y: 2, z: 4, core: 2. Of those that a mesh axis runs over, the one named last changes fastest.
Arguments:
- tokens: float32 [25088, 384], P(('dp', 'head')), may hold values from -6 to 6
- outputs_grad: bfloat16 [25088, 384], P(('dp', 'head')), may hold values from -6 to 6
- image_kind: int32 [8, 16], P('dp'), may hold values from 0 to 2, as said below
- qkv_weight: bfloat16 [2, 384, 3, 384], P(None, None, None, 'head'), may hold values from -0.3125 to 0.3125
- qv_bias: float32 [2, 2, 384], P(None, None, 'head'), may hold values from -3 to 3
- bias_table: float32 [2, 169, 12], P(None, None, 'head'), may hold values from -4 to 4
- proj_weight: bfloat16 [2, 384, 384], P(None, 'head'), may hold values from -1.25 to 1.25
- fc1_weight: bfloat16 [2, 384, 1536], P(None, None, 'head'), may hold values from -0.3125 to 0.3125
- fc1_bias: float32 [2, 1536], P(None, 'head'), may hold values from -3 to 3
- fc2_weight: bfloat16 [2, 1536, 384], P(None, 'head'), may hold values from -0.15625 to 0.15625
- gains: float32 [2, 2, 384], replicated, may hold values from 0.5 to 1.5
- shifts: float32 [2, 4, 384], replicated, may hold values from -2 to 2
Outputs:
- outputs: float32 [25088, 384], P(('dp', 'head'))
- tokens_grad: float32 [25088, 384], P(('dp', 'head'))
- qkv_weight_grad: float32 [2, 384, 3, 384], P(None, None, None, 'head')
- qv_bias_grad: float32 [2, 2, 384], P(None, None, 'head')
- bias_table_grad: float32 [2, 169, 12], P(None, None, 'head')
- proj_weight_grad: float32 [2, 384, 384], P(None, 'head')
- fc1_weight_grad: float32 [2, 384, 1536], P(None, None, 'head')
- fc1_bias_grad: float32 [2, 1536], P(None, 'head')
- fc2_weight_grad: float32 [2, 1536, 384], P(None, 'head')
- gains_grad: float32 [2, 2, 384], replicated
- shifts_grad: float32 [2, 4, 384], replicated
Inputs may be any that keep to these rules, and one draw needn't show every extreme that they name: `image_kind`: row d lists the images of dp index d: 1 a 14 x 14 map in 4 windows, 2 a 21 x 21 map in 9 windows, 0 none. Zeros only follow images, the first entry is an image, a row's windows total at most 64 and fill slots from the first on; the remaining slots are empty. Some row is filled exactly, by images of kind 1.
All inputs are finite; a program needn't handle non-finite values.
Results may differ from a plain program's by a relative error of at most 0.03.
Values may be sent and summed in bfloat16 or wider, within the bound.
No kernel may reach another device: no remote copies, remote signals or barrier semaphores. Data moves between devices by JAX's collectives and lax.ppermute only.
A program may use at most 192 MiB of HBM per device.

v0:
```python
import jax
import jax.numpy as jnp
from jax import lax
from jax.sharding import PartitionSpec as P

D = 384
HEADS = 12
LAYERS = 2


ln_eps = 1e-05
mask_fill = -100.0
highest = lax.Precision.HIGHEST


def window_plan(image_kinds, slot_count, offset):
    counts = jnp.where(image_kinds == 2, 9, jnp.where(image_kinds == 1, 4, 0)).astype(jnp.int32)
    end_slots = jnp.cumsum(counts)
    starts = end_slots - counts
    side_count = jnp.where(image_kinds == 2, 3, 2).astype(jnp.int32)
    slot_ids = jnp.arange(slot_count, dtype=jnp.int32)
    inside = (slot_ids[:, None] >= starts[None, :]) & (slot_ids[:, None] < end_slots[None, :])
    live_slots = jnp.any(inside, axis=1)
    first_slot = jnp.sum(jnp.where(inside, starts[None, :], 0), axis=1)
    image_side = jnp.maximum(jnp.sum(jnp.where(inside, side_count[None, :], 0), axis=1), 1)
    local_slot = slot_ids - first_slot
    map_span = (image_side * 7)[:, None]
    places = jnp.arange(49, dtype=jnp.int32)
    image_row = (local_slot // image_side)[:, None] * 7 + (places // 7)[None, :]
    image_col = (local_slot % image_side)[:, None] * 7 + (places % 7)[None, :]
    from_row = (image_row + offset + map_span) % map_span
    from_col = (image_col + offset + map_span) % map_span
    source = (
        (first_slot[:, None] + from_row // 7 * image_side[:, None] + from_col // 7) * 49
        + from_row % 7 * 7
        + from_col % 7
    )
    same_row = slot_ids[:, None] * 49 + places[None, :]
    source = jnp.where(live_slots[:, None], source, same_row)
    band_row = (image_row >= map_span - 7).astype(jnp.int32) + (image_row >= map_span - 3).astype(
        jnp.int32
    )
    band_col = (image_col >= map_span - 7).astype(jnp.int32) + (image_col >= map_span - 3).astype(
        jnp.int32
    )
    region = jnp.where(live_slots[:, None], band_row * 3 + band_col, 0)
    return (source.reshape(-1), region, live_slots)


def relative_index():
    places = jnp.arange(49, dtype=jnp.int32)
    place_row = places // 7
    place_col = places % 7
    return (
        (place_row[:, None] - place_row[None, :] + 6) * 13
        + place_col[:, None]
        - place_col[None, :]
        + 6
    )


def norm_stats(values):
    average = jnp.mean(values, axis=-1, keepdims=True)
    centred = values - average
    inverse_std = lax.rsqrt(jnp.mean(centred * centred, axis=-1, keepdims=True) + ln_eps)
    return (centred * inverse_std, inverse_std)


def norm_back(incoming, scaled, inverse_std, gain_row):
    weighted = incoming * gain_row
    return inverse_std * (
        weighted
        - jnp.mean(weighted, axis=-1, keepdims=True)
        - scaled * jnp.mean(weighted * scaled, axis=-1, keepdims=True)
    )


def gelu_exact(values):
    return jax.nn.gelu(values, approximate=False)


def score_block(queries, keys_low, table_bias, mask_now, score_scale):
    scores = (
        jnp.einsum("wphe,wqhe->whpq", queries, keys_low, preferred_element_type=jnp.float32)
        * score_scale
    )
    return scores + table_bias[None] + mask_now[:, None]


def attend(queries, keys_low, values_low, table_bias, mask_now, score_scale):
    scores = score_block(queries, keys_low, table_bias, mask_now, score_scale)
    top_score = jnp.max(scores, axis=-1, keepdims=True)
    exponent = jnp.exp(scores - top_score)
    totals = jnp.sum(exponent, axis=-1, keepdims=True)
    attn_probs = (exponent / totals).astype(jnp.bfloat16)
    attended = jnp.einsum(
        "whpq,wqhe->wphe", attn_probs, values_low, preferred_element_type=jnp.float32
    )
    return (attended, top_score + jnp.log(totals))


def attend_back(
    queries, keys_low, values_low, table_bias, mask_now, score_scale, log_total, upstream
):
    scores = score_block(queries, keys_low, table_bias, mask_now, score_scale)
    attn_probs = jnp.exp(scores - log_total)
    value_grad = jnp.einsum(
        "whpq,wphe->wqhe",
        attn_probs.astype(jnp.bfloat16),
        upstream,
        preferred_element_type=jnp.float32,
    )
    prob_grad = jnp.einsum(
        "wphe,wqhe->whpq", upstream, values_low, preferred_element_type=jnp.float32
    )
    score_grad = (
        attn_probs * (prob_grad - jnp.sum(prob_grad * attn_probs, axis=-1, keepdims=True))
    ).astype(jnp.bfloat16)
    query_grad = (
        jnp.einsum("whpq,wqhe->wphe", score_grad, keys_low, preferred_element_type=jnp.float32)
        * score_scale
    )
    key_grad = (
        jnp.einsum("whpq,wphe->wqhe", score_grad, queries, preferred_element_type=jnp.float32)
        * score_scale
    )
    bias_grad = jnp.sum(score_grad.astype(jnp.float32), axis=0)
    return (query_grad, key_grad, value_grad, bias_grad)


def body(
    tokens,
    outputs_grad,
    image_kind,
    qkv_weight,
    qv_bias,
    bias_table,
    proj_weight,
    fc1_weight,
    fc1_bias,
    fc2_weight,
    gains,
    shifts,
):
    low_type = jnp.bfloat16
    wide_type = jnp.float32
    own_rows = tokens.shape[0]
    group_rows = own_rows * lax.axis_size("head")
    slot_count = group_rows // 49
    row_start = lax.axis_index("head") * own_rows
    head_dim = D // HEADS
    score_scale = head_dim ** (-0.5)
    local_width = qkv_weight.shape[3]
    local_heads = local_width // head_dim
    source, region, live_slots = window_plan(image_kind[0], slot_count, 3)
    inverse = window_plan(image_kind[0], slot_count, -3)[0]
    shift_mask = jnp.where(region[:, :, None] != region[:, None, :], mask_fill, 0.0).astype(
        wide_type
    )
    plain_mask = jnp.zeros_like(shift_mask)
    row_live = jnp.repeat(live_slots.astype(wide_type), 49)[:, None]
    one_hot = (
        relative_index().reshape(-1)[:, None] == jnp.arange(169, dtype=jnp.int32)[None, :]
    ).astype(wide_type)
    window_shape = (group_rows // 49, 49, local_heads, head_dim)

    def norm_rows(values):
        return lax.all_gather(values, "head", axis=0, tiled=True)

    def grad_rows(values):
        return lax.all_gather(values, "head", axis=0, tiled=True)

    def branch_total(product):
        return lax.psum_scatter(
            product(jnp.int32(0), lax.axis_size("head") * own_rows).astype(jnp.bfloat16),
            "head",
            scatter_dimension=0,
            tiled=True,
        ).astype(jnp.float32)

    def input_total(product):
        return lax.psum_scatter(
            product(jnp.int32(0), lax.axis_size("head") * own_rows).astype(jnp.bfloat16),
            "head",
            scatter_dimension=0,
            tiled=True,
        ).astype(jnp.float32)

    def table_bias(layer_index):
        looked = jnp.dot(one_hot, bias_table[layer_index], precision=highest)
        return jnp.transpose(looked.reshape(49, 49, local_heads), (2, 0, 1))

    hidden = tokens
    cotangent = outputs_grad.astype(wide_type)
    live_held = lax.dynamic_slice_in_dim(row_live, row_start, own_rows, 0)
    saved_layers = []
    for layer_index in range(LAYERS):
        shifted = layer_index % 2 == 1
        mask_now = shift_mask if shifted else plain_mask
        scaled_attn, recip_attn = norm_stats(hidden)
        normed = (scaled_attn * gains[layer_index, 0] + shifts[layer_index, 0]).astype(low_type)
        normed_all = norm_rows(normed)
        if shifted:
            normed_view = jnp.take(normed_all, source, axis=0)
        else:
            normed_view = normed_all
        project = jnp.einsum(
            "rd,dce->rce", normed_view, qkv_weight[layer_index], preferred_element_type=wide_type
        )
        queries = (project[:, 0] + qv_bias[layer_index, 0]).astype(low_type).reshape(window_shape)
        keys_low = project[:, 1].astype(low_type).reshape(window_shape)
        values_low = (
            (project[:, 2] + qv_bias[layer_index, 1]).astype(low_type).reshape(window_shape)
        )
        attended, log_total = attend(
            queries, keys_low, values_low, table_bias(layer_index), mask_now, score_scale
        )
        attended = attended.reshape(group_rows, local_width).astype(low_type)
        if shifted:
            attended = jnp.take(attended, inverse, axis=0)
        proj_now = proj_weight[layer_index]

        def proj_product(first_row, row_count):
            return jnp.dot(attended, proj_now, preferred_element_type=wide_type)

        middle = hidden + branch_total(proj_product) + shifts[layer_index, 2]
        scaled_mlp, recip_mlp = norm_stats(middle)
        normed_mlp = (scaled_mlp * gains[layer_index, 1] + shifts[layer_index, 1]).astype(low_type)
        normed_mlp_all = norm_rows(normed_mlp)
        preact = (
            jnp.dot(normed_mlp_all, fc1_weight[layer_index], preferred_element_type=wide_type)
            + fc1_bias[layer_index]
        )
        active = gelu_exact(preact).astype(low_type)
        fc2_now = fc2_weight[layer_index]

        def mlp_product(first_row, row_count):
            return jnp.dot(active, fc2_now, preferred_element_type=wide_type)

        hidden = middle + branch_total(mlp_product) + shifts[layer_index, 3]
        saved_layers.append(
            (
                scaled_attn,
                recip_attn,
                normed_all,
                queries,
                keys_low,
                values_low,
                log_total,
                attended,
                scaled_mlp,
                recip_mlp,
                normed_mlp_all,
                preact,
                active,
            )
        )
    output = hidden * live_held
    gradient = cotangent * live_held
    weight_list = [None] * LAYERS
    gain_list = [None] * LAYERS
    shift_list = [None] * LAYERS
    for layer_index in reversed(range(LAYERS)):
        (
            scaled_attn,
            recip_attn,
            normed_all,
            queries,
            keys_low,
            values_low,
            log_total,
            attended,
            scaled_mlp,
            recip_mlp,
            normed_mlp_all,
            preact,
            active,
        ) = saved_layers[layer_index]
        shifted = layer_index % 2 == 1
        mask_now = shift_mask if shifted else plain_mask
        fc2_in = gradient.astype(low_type)
        fc2_shift = jnp.sum(fc2_in.astype(wide_type), axis=0)
        fc2_all = grad_rows(fc2_in)
        fc2_grad = jnp.einsum("rf,rd->fd", active, fc2_all, preferred_element_type=wide_type)
        active_grad = jnp.einsum(
            "rd,fd->rf", fc2_all, fc2_weight[layer_index], preferred_element_type=wide_type
        )
        gelu_value, slope_pull = jax.vjp(gelu_exact, preact)
        preact_grad = slope_pull(active_grad)[0].astype(low_type)
        fc1_shift = jnp.sum(preact_grad.astype(wide_type), axis=0)
        fc1_grad = jnp.einsum(
            "rd,rf->df", normed_mlp_all, preact_grad, preferred_element_type=wide_type
        )
        fc1_now = fc1_weight[layer_index]

        def mlp_back(first_row, row_count):
            return jnp.einsum("rf,df->rd", preact_grad, fc1_now, preferred_element_type=wide_type)

        normed_mlp_grad = input_total(mlp_back)
        gain_mlp = jnp.sum(normed_mlp_grad * scaled_mlp, axis=0)
        shift_mlp = jnp.sum(normed_mlp_grad, axis=0)
        gradient = gradient + norm_back(
            normed_mlp_grad, scaled_mlp, recip_mlp, gains[layer_index, 1]
        )
        proj_in = gradient.astype(low_type)
        proj_shift = jnp.sum(proj_in.astype(wide_type), axis=0)
        proj_all = grad_rows(proj_in)
        proj_grad = jnp.einsum("re,rd->ed", attended, proj_all, preferred_element_type=wide_type)
        attended_grad = jnp.einsum(
            "rd,ed->re", proj_all, proj_weight[layer_index], preferred_element_type=wide_type
        ).astype(low_type)
        if shifted:
            attended_grad = jnp.take(attended_grad, source, axis=0)
        query_grad, key_grad, value_grad, bias_grad = attend_back(
            queries,
            keys_low,
            values_low,
            table_bias(layer_index),
            mask_now,
            score_scale,
            log_total,
            attended_grad.reshape(window_shape),
        )
        stacked = jnp.stack(
            [
                query_grad.reshape(group_rows, local_width),
                key_grad.reshape(group_rows, local_width),
                value_grad.reshape(group_rows, local_width),
            ],
            axis=1,
        ).astype(low_type)
        if shifted:
            stacked = jnp.take(stacked, inverse, axis=0)
        qkv_grad = jnp.einsum("rd,rce->dce", normed_all, stacked, preferred_element_type=wide_type)
        qv_grad = jnp.sum(stacked[:, 0::2].astype(wide_type), axis=0)
        table_grad = jnp.einsum(
            "nt,nh->th",
            one_hot,
            jnp.transpose(bias_grad, (1, 2, 0)).reshape(2401, local_heads),
            precision=highest,
        )
        qkv_now = qkv_weight[layer_index]

        def attn_back(first_row, row_count):
            return jnp.einsum("rce,dce->rd", stacked, qkv_now, preferred_element_type=wide_type)

        normed_grad = input_total(attn_back)
        gain_attn = jnp.sum(normed_grad * scaled_attn, axis=0)
        shift_attn = jnp.sum(normed_grad, axis=0)
        gradient = gradient + norm_back(normed_grad, scaled_attn, recip_attn, gains[layer_index, 0])
        weight_list[layer_index] = (
            qkv_grad,
            qv_grad,
            table_grad,
            proj_grad,
            fc1_grad,
            fc1_shift,
            fc2_grad,
        )
        gain_list[layer_index] = jnp.stack([gain_attn, gain_mlp])
        shift_list[layer_index] = jnp.stack([shift_attn, shift_mlp, proj_shift, fc2_shift])
    qkv_total = jnp.stack([weight_list[layer_index][0] for layer_index in range(LAYERS)])
    qv_total = jnp.stack([weight_list[layer_index][1] for layer_index in range(LAYERS)])
    table_total = jnp.stack([weight_list[layer_index][2] for layer_index in range(LAYERS)])
    proj_total = jnp.stack([weight_list[layer_index][3] for layer_index in range(LAYERS)])
    fc1_total = jnp.stack([weight_list[layer_index][4] for layer_index in range(LAYERS)])
    fc1_bias_total = jnp.stack([weight_list[layer_index][5] for layer_index in range(LAYERS)])
    fc2_total = jnp.stack([weight_list[layer_index][6] for layer_index in range(LAYERS)])
    qkv_total, qv_total, table_total, proj_total, fc1_total, fc1_bias_total, fc2_total = lax.psum(
        (qkv_total, qv_total, table_total, proj_total, fc1_total, fc1_bias_total, fc2_total), "dp"
    )
    gain_total, shift_total = lax.psum(
        (jnp.stack(gain_list), jnp.stack(shift_list)), ("dp", "head")
    )
    return (
        output,
        gradient,
        qkv_total,
        qv_total,
        table_total,
        proj_total,
        fc1_total,
        fc1_bias_total,
        fc2_total,
        gain_total,
        shift_total,
    )


def solution(mesh):
    placed = (
        P(("dp", "head"), None),
        P(("dp", "head"), None),
        P("dp", None),
        P(None, None, None, "head"),
        P(None, None, "head"),
        P(None, None, "head"),
        P(None, "head", None),
        P(None, None, "head"),
        P(None, "head"),
        P(None, "head", None),
        P(),
        P(),
    )
    return jax.shard_map(
        body,
        mesh=mesh,
        in_specs=placed,
        out_specs=(
            P(("dp", "head"), None),
            P(("dp", "head"), None),
            P(None, None, None, "head"),
            P(None, None, "head"),
            P(None, None, "head"),
            P(None, "head", None),
            P(None, None, "head"),
            P(None, "head"),
            P(None, "head", None),
            P(),
            P(),
        ),
        check_vma=False,
    )
```

profile of v0, /device:TPU:0, one launch (start us, length us, event | category | flops | bytes accessed | tf_op | source)
XLA Modules:
  0.0 963.2 jit_solution(4668483861173813809)
XLA Ops:
  16.8 22.8 %all-gather.9.cloned.1.call-done = bf16[3136,384]{1,0:T(8,128)(2,1)} async-done(((bf16[784,384]{1,0:T(8,128)(2,1)}), bf16[3136,384]{1,0:T(8,128)(2,1)}) %all-gather.9.cloned.1.call-update) | async-done | bytes 2408464 | tf_op jit(solution)/shard_map/all_gather | solution.py:168
  44.1 4.6 convert_element_type.240
  48.7 7.0 squeeze.57
  55.7 6.8 squeeze.58
  65.7 4.1 fusion.244
  79.8 33.5 %reduce-scatter.9.cloned.1.call-done = bf16[784,384]{1,0:T(8,128)(2,1)} async-done(((bf16[3136,384]{1,0:T(8,128)(2,1)}), bf16[784,384]{1,0:T(8,128)(2,1)}) %reduce-scatter.9.cloned.1.call-update) | async-done | bytes 602128 | tf_op jit(solution)/shard_map/reduce_scatter | solution.py:174
  116.2 24.4 %all-gather.11.cloned.1.call-done = bf16[3136,384]{1,0:T(8,128)(2,1)} async-done(((bf16[784,384]{1,0:T(8,128)(2,1)}), bf16[3136,384]{1,0:T(8,128)(2,1)}) %all-gather.11.cloned.1.call-update) | async-done | bytes 2408464 | tf_op jit(solution)/shard_map/all_gather | solution.py:168
  140.6 15.1 %multiply_convert_fusion.3 = (bf16[3136,384]{1,0:T(8,128)(2,1)S(1)}, f32[3136,384]{1,0:T(8,128)}, f32[3136,384]{1,0:T(8,128)}) fusion(f32[384]{0:T(512)S(1)} %get-tuple-element.97, bf16[3136,384]{1,0:T(8,128)(2,1)} %all-gather.11.cloned.1.call-done, bf16[2,384,384]{2,1,0:T(8,128)(2,1)S(1)} %copy-done.57), kind=kOutput, calls=%fused_computation.53 | convolution fusion | flops 1004322816 | bytes 14747648 | tf_op jit(solution)/shard_map/dot_general | solution.py:231
  157.2 3.1 convolution_convert_fusion.4
  160.4 33.5 %reduce-scatter.11.cloned.1.call-done = bf16[784,384]{1,0:T(8,128)(2,1)} async-done(((bf16[3136,384]{1,0:T(8,128)(2,1)}), bf16[784,384]{1,0:T(8,128)(2,1)}) %reduce-scatter.11.cloned.1.call-update) | async-done | bytes 602128 | tf_op jit(solution)/shard_map/reduce_scatter | solution.py:174
  204.0 17.8 %all-gather.13.cloned.1.call-done = bf16[3136,384]{1,0:T(8,128)(2,1)} async-done(((bf16[784,384]{1,0:T(8,128)(2,1)}), bf16[3136,384]{1,0:T(8,128)(2,1)}) %all-gather.13.cloned.1.call-update) | async-done | bytes 2408464 | tf_op jit(solution)/shard_map/all_gather | solution.py:168
  221.8 11.4 %gather_fusion = bf16[3136,384]{1,0:T(8,128)(2,1)} fusion(bf16[3136,384]{1,0:T(8,128)(2,1)} %all-gather.13.cloned.1.call-done, s32[4096]{0:T(1024)S(1)} %pad_clamp_fusion.3), kind=kCustom, calls=%fused_computation.2 | custom fusion | bytes 4829440 | tf_op jit(solution)/shard_map/jit(_take)/gather | solution.py:204
  233.3 3.6 fusion.33
  238.2 5.4 convert_element_type.254
  243.6 6.6 squeeze.64
  250.2 5.7 squeeze.65
  261.3 4.3 fusion.245
  272.2 3.0 convert_element_type.262
  275.7 6.7 gather_fusion.2
  282.4 3.1 convolution_convert_fusion.3
  286.0 33.0 %reduce-scatter.13.cloned.1.call-done = bf16[784,384]{1,0:T(8,128)(2,1)} async-done(((bf16[3136,384]{1,0:T(8,128)(2,1)}), bf16[784,384]{1,0:T(8,128)(2,1)}) %reduce-scatter.13.cloned.1.call-update) | async-done | bytes 602128 | tf_op jit(solution)/shard_map/reduce_scatter | solution.py:174
  324.6 22.4 %all-gather.15.cloned.1.call-done = bf16[3136,384]{1,0:T(8,128)(2,1)} async-done(((bf16[784,384]{1,0:T(8,128)(2,1)}), bf16[3136,384]{1,0:T(8,128)(2,1)}) %all-gather.15.cloned.1.call-update) | async-done | bytes 2408464 | tf_op jit(solution)/shard_map/all_gather | solution.py:168
  347.0 15.0 %multiply_convert_fusion.2 = (bf16[3136,384]{1,0:T(8,128)(2,1)}, f32[3136,384]{1,0:T(8,128)}, f32[3136,384]{1,0:T(8,128)}) fusion(f32[384]{0:T(512)S(1)} %get-tuple-element.96, bf16[3136,384]{1,0:T(8,128)(2,1)} %all-gather.15.cloned.1.call-done, bf16[2,384,384]{2,1,0:T(8,128)(2,1)S(1)} %copy-done.58), kind=kOutput, calls=%fused_computation.40 | convolution fusion | flops 1004322816 | bytes 14747648 | tf_op jit(solution)/shard_map/dot_general | solution.py:231
  362.0 11.6 %all-gather.17.cloned.1.call-done = bf16[3136,384]{1,0:T(8,128)(2,1)} async-done(((bf16[784,384]{1,0:T(8,128)(2,1)}), bf16[3136,384]{1,0:T(8,128)(2,1)}) %all-gather.17.cloned.1.call-update) | async-done | bytes 2408464 | tf_op jit(solution)/shard_map/all_gather | solution.py:171
  373.6 8.3 convert_reduce_fusion.2
  383.4 3.1 convolution_convert_fusion.1
  386.5 4.7 convolution_convert_fusion.2
  391.3 28.7 %reduce-scatter.17.cloned.1.call-done = bf16[784,384]{1,0:T(8,128)(2,1)} async-done(((bf16[3136,384]{1,0:T(8,128)(2,1)}), bf16[784,384]{1,0:T(8,128)(2,1)}) %reduce-scatter.17.cloned.1.call-update) | async-done | bytes 602128 | tf_op jit(solution)/shard_map/reduce_scatter | solution.py:182
  421.8 34.0 %reduce-scatter.15.cloned.1.call-done = bf16[784,384]{1,0:T(8,128)(2,1)} async-done(((bf16[3136,384]{1,0:T(8,128)(2,1)}), bf16[784,384]{1,0:T(8,128)(2,1)}) %reduce-scatter.15.cloned.1.call-update) | async-done | bytes 602128 | tf_op jit(solution)/shard_map/reduce_scatter | solution.py:174
  455.8 3.2 convert_reduce_fusion.11
  460.2 23.3 %all-gather.19.cloned.1.call-done = bf16[3136,384]{1,0:T(8,128)(2,1)} async-done(((bf16[784,384]{1,0:T(8,128)(2,1)}), bf16[3136,384]{1,0:T(8,128)(2,1)}) %all-gather.19.cloned.1.call-update) | async-done | bytes 2408464 | tf_op jit(solution)/shard_map/all_gather | solution.py:171
  486.4 6.7 gather_fusion.3
  495.1 5.7 reshape.752
  500.8 5.1 fusion.61
  506.0 5.3 multiply_reduce_fusion.1
  516.5 3.3 fusion.64
  521.9 3.0 stack_reshape.26
  524.9 2.9 copy.221
  527.8 3.2 copy.212
  531.0 3.0 stack_reshape.24
  534.1 3.2 copy.215
  537.3 3.0 stack_reshape.25
  546.1 8.9 pad_maximum_fusion
  555.0 13.5 %gather_fusion.1 = bf16[3136,3,96]{2,1,0:T(4,128)(2,1)} fusion(bf16[3136,3,96]{2,1,0:T(4,128)(2,1)} %pad_maximum_fusion, s32[4096]{0:T(1024)S(1)} %pad_clamp_fusion), kind=kCustom, calls=%fused_computation.3 | custom fusion | bytes 3625216 | tf_op jit(solution)/shard_map/jit(_take)/gather | solution.py:333
  568.5 13.4 %broadcast_select_fusion = bf16[3136,3,96]{2,1,0:T(4,128)(2,1)} fusion(bf16[3136,3,96]{2,1,0:T(4,128)(2,1)} %gather_fusion.1, pred[3136]{0:T(1024)(128)(4,1)S(1)} %compare_and_fusion), kind=kLoop, calls=%fused_computation.74 | loop fusion | flops 903168 | bytes 3615808 | tf_op jit(solution)/shard_map/jit(_take)/select_n | solution.py:333
  581.9 5.9 copy.222
  587.9 4.6 fusion
  592.5 33.5 %reduce-scatter.19.cloned.1.call-done = bf16[784,384]{1,0:T(8,128)(2,1)} async-done(((bf16[3136,384]{1,0:T(8,128)(2,1)}), bf16[784,384]{1,0:T(8,128)(2,1)}) %reduce-scatter.19.cloned.1.call-update) | async-done | bytes 602128 | tf_op jit(solution)/shard_map/reduce_scatter | solution.py:182
  631.4 24.5 %all-gather.21.cloned.1.call-done = bf16[3136,384]{1,0:T(8,128)(2,1)} async-done(((bf16[784,384]{1,0:T(8,128)(2,1)}), bf16[3136,384]{1,0:T(8,128)(2,1)}) %all-gather.21.cloned.1.call-update) | async-done | bytes 2408464 | tf_op jit(solution)/shard_map/all_gather | solution.py:171
  655.9 7.8 convert_reduce_fusion.3
  665.1 3.1 convolution_convert_fusion
  668.3 33.5 %reduce-scatter.21.cloned.1.call-done = bf16[784,384]{1,0:T(8,128)(2,1)} async-done(((bf16[3136,384]{1,0:T(8,128)(2,1)}), bf16[784,384]{1,0:T(8,128)(2,1)}) %reduce-scatter.21.cloned.1.call-update) | async-done | bytes 602128 | tf_op jit(solution)/shard_map/reduce_scatter | solution.py:182
  707.2 23.7 %all-gather.23.cloned.1.call-done = bf16[3136,384]{1,0:T(8,128)(2,1)} async-done(((bf16[784,384]{1,0:T(8,128)(2,1)}), bf16[3136,384]{1,0:T(8,128)(2,1)}) %all-gather.23.cloned.1.call-update) | async-done | bytes 2408464 | tf_op jit(solution)/shard_map/all_gather | solution.py:171
  733.5 4.8 reshape.754
  738.3 4.6 fusion.58
  743.0 5.3 multiply_reduce_fusion
  751.7 3.3 fusion.66
  767.6 3.1 fusion.1
  771.0 4.0 convolution_bitcast_fusion.2
  793.1 35.3 %slice.159 = bf16[3136,2,96]{2,1,0:T(2,128)(2,1)} slice(bf16[3136,3,96]{2,1,0:T(4,128)(2,1)S(1)} %copy-done.12), slice={[0:3136:1], [0:3:2], [0:96:1]} | slice | bytes 2408448 | tf_op jit(solution)/shard_map/slice | solution.py:335
  829.6 4.5 convert_reduce_fusion.4
  837.0 38.7 %all-reduce.1 = (f32[2,2,96]{2,1,0:T(2,128)}, f32[2,169,3]{1,2,0:T(4,128)S(1)}, f32[2,384]{1,0:T(2,128)}) all-reduce(f32[2,2,96]{2,1,0:T(2,128)S(1)} %pad_maximum_fusion.9, f32[2,169,3]{1,2,0:T(4,128)S(1)} %pad_maximum_fusion.6, f32[2,384]{1,0:T(2,128)S(1)} %pad_maximum_fusion.8), channel_id=1, replica_groups=mesh['dp'=8,'head'=4] {'dp'}, use_global_device_ids=true, to_apply=%region_37.40 | all-reduce | flops 2166 | bytes 17328 | tf_op jit(solution)/shard_map/psum | solution.py:369
  878.2 37.8 %all-reduce = (f32[2,2,384]{2,1,0:T(2,128)}, f32[2,4,384]{2,1,0:T(4,128)}) all-reduce(f32[2,2,384]{2,1,0:T(2,128)S(1)} %pad_maximum_fusion.7, f32[2,4,384]{2,1,0:T(4,128)S(1)} %pad_maximum_fusion.5), channel_id=1, replica_groups=mesh['dp'=8,'head'=4] {'dp','head'}, use_global_device_ids=true, to_apply=%region_51.54 | all-reduce | flops 4608 | bytes 36864 | tf_op jit(solution)/shard_map/psum | solution.py:372
  918.7 31.6 %all-reduce.5.cloned.1.call-done = (f32[2,384,3,96]{1,3,2,0:T(8,128)}, f32[2,96,384]{2,1,0:T(8,128)}, f32[2,384,384]{2,1,0:T(8,128)}, f32[2,384,384]{2,1,0:T(8,128)}) async-done(((f32[2,384,3,96]{1,3,2,0:T(8,128)}, f32[2,96,384]{2,1,0:T(8,128)}, f32[2,384,384]{2,1,0:T(8,128)}, f32[2,384,384]{2,1,0:T(8,128)}), (f32[2,384,3,96]{1,3,2,0:T(8,128)}, f32[2,96,384]{2,1,0:T(8,128)}, f32[2,384,384]{2,1,0:T(8,128)}, ...) | async-done | bytes 3538960 | tf_op jit(solution)/shard_map/psum | solution.py:369
  (446 shorter events, 147.2 us)
Async XLA Ops:
  7.2 5.2 copy-start.107
  7.2 6.0 copy-start.98
  7.2 32.3 %all-gather.9.cloned.1.call-start = ((), (), s32[]{:S(2)}) async-start(), calls=%async_computation.8 | async-start | bytes 3010560 | tf_op jit(solution)/shard_map/all_gather | solution.py:168
  8.8 7.2 copy-start.68
  11.2 103.7 %copy-start.85 = (f32[384]{0:T(512)}, f32[384]{0:T(512)S(1)}, u32[]{:S(2)}) copy-start(f32[384]{0:T(512)S(1)} %get-tuple-element.178) | copy-start | bytes 4612
  12.4 100.9 %reduce-scatter.9.cloned.1.call-start = ((), (), s32[]{:S(2)}) async-start(), calls=%async_computation.9 | async-start | bytes 3010560 | tf_op jit(solution)/shard_map/reduce_scatter | solution.py:174
  48.7 17.0 %copy-start.18 = (bf16[64,49,3,32]{1,0,3,2:T(8,128)(2,1)}, bf16[64,49,3,32]{1,0,3,2:T(8,128)(2,1)S(1)}, u32[]{:S(2)}) copy-start(bf16[64,49,3,32]{1,0,3,2:T(8,128)(2,1)S(1)} %convert_element_type.240) | copy-start | bytes 1806340
  65.4 6.2 copy-start.31
  77.4 35.8 %copy-start.96 = (f32[384]{0:T(512)S(1)}, f32[384]{0:T(512)}, u32[]{:S(2)}) copy-start(f32[384]{0:T(512)} %get-tuple-element.89) | copy-start | bytes 4612
  79.7 35.3 %copy-start.95 = (f32[384]{0:T(512)S(1)}, f32[384]{0:T(512)}, u32[]{:S(2)}) copy-start(f32[384]{0:T(512)} %get-tuple-element.88) | copy-start | bytes 4612
  79.7 60.9 %all-gather.11.cloned.1.call-start = ((), (), s32[]{:S(2)}) async-start(), calls=%async_computation.10 | async-start | bytes 3010560 | tf_op jit(solution)/shard_map/all_gather | solution.py:168
  114.6 26.1 %copy-start.57 = (bf16[2,384,384]{2,1,0:T(8,128)(2,1)S(1)}, bf16[2,384,384]{2,1,0:T(8,128)(2,1)}, u32[]{:S(2)}) copy-start(bf16[2,384,384]{2,1,0:T(8,128)(2,1)} %param.23) | copy-start | bytes 1769476
  114.6 26.0 %copy-start.77 = (f32[784]{0:T(1024)}, f32[784]{0:T(1024)S(1)}, u32[]{:S(2)}) copy-start(f32[784]{0:T(1024)S(1)} %broadcast_multiply_fusion.10) | copy-start | bytes 9412
  114.9 25.7 %copy-start.81 = (f32[784]{0:T(1024)}, f32[784]{0:T(1024)S(1)}, u32[]{:S(2)}) copy-start(f32[784]{0:T(1024)S(1)} %add_rsqrt_fusion.2) | copy-start | bytes 9412
  116.1 77.7 %reduce-scatter.11.cloned.1.call-start = ((), (), s32[]{:S(2)}) async-start(), calls=%async_computation.11 | async-start | bytes 3010560 | tf_op jit(solution)/shard_map/reduce_scatter | solution.py:174
  140.6 16.6 %copy-start.62 = (bf16[2,384,384]{2,1,0:T(8,128)(2,1)S(1)}, bf16[2,384,384]{2,1,0:T(8,128)(2,1)}, u32[]{:S(2)}) copy-start(bf16[2,384,384]{2,1,0:T(8,128)(2,1)} %param.25) | copy-start | bytes 1769476
  160.3 33.5 %copy-start.94 = (f32[384]{0:T(512)S(1)}, f32[384]{0:T(512)}, u32[]{:S(2)}) copy-start(f32[384]{0:T(512)} %get-tuple-element.87) | copy-start | bytes 4612
  160.3 35.9 %copy-start.93 = (f32[384]{0:T(512)S(1)}, f32[384]{0:T(512)}, u32[]{:S(2)}) copy-start(f32[384]{0:T(512)} %get-tuple-element.86) | copy-start | bytes 4612
  160.3 61.5 %all-gather.13.cloned.1.call-start = ((), (), s32[]{:S(2)}) async-start(), calls=%async_computation.12 | async-start | bytes 3010560 | tf_op jit(solution)/shard_map/all_gather | solution.py:168
  197.3 121.7 %reduce-scatter.13.cloned.1.call-start = ((), (), s32[]{:S(2)}) async-start(), calls=%async_computation.13 | async-start | bytes 3010560 | tf_op jit(solution)/shard_map/reduce_scatter | solution.py:174
  197.7 35.5 %copy-start.110 = (pred[64]{0:T(512)(128)(4,1)}, pred[64]{0:T(512)(128)(4,1)S(1)}, u32[]{:S(2)}) copy-start(pred[64]{0:T(512)(128)(4,1)S(1)} %fusion.219) | copy-start | bytes 196
  204.0 29.3 %copy-start.56 = (bf16[1,384,3,96]{1,3,2,0:T(8,128)(2,1)S(1)}, bf16[1,384,3,96]{1,3,2,0:T(8,128)(2,1)}, u32[]{:S(2)}) copy-start(bf16[1,384,3,96]{1,3,2,0:T(8,128)(2,1)} %get-tuple-element.143) | copy-start | bytes 663556
  258.8 8.6 copy-start.33
  282.4 36.6 %copy-start.6 = (f32[784,384]{1,0:T(8,128)S(1)}, f32[784,384]{1,0:T(8,128)}, u32[]{:S(2)}) copy-start(f32[784,384]{1,0:T(8,128)} %copy-done.5) | copy-start | bytes 3612676
  282.4 36.6 %copy-start.92 = (f32[384]{0:T(512)S(1)}, f32[384]{0:T(512)}, u32[]{:S(2)}) copy-start(f32[384]{0:T(512)} %get-tuple-element.85) | copy-start | bytes 4612
  285.5 35.9 %copy-start.87 = (f32[384]{0:T(512)S(1)}, f32[384]{0:T(512)}, u32[]{:S(2)}) copy-start(f32[384]{0:T(512)} %get-tuple-element.179) | copy-start | bytes 4612
  285.5 35.9 %copy-start.91 = (f32[384]{0:T(512)S(1)}, f32[384]{0:T(512)}, u32[]{:S(2)}) copy-start(f32[384]{0:T(512)} %get-tuple-element.91) | copy-start | bytes 4612
  285.5 61.5 %all-gather.15.cloned.1.call-start = ((), (), s32[]{:S(2)}) async-start(), calls=%async_computation.14 | async-start | bytes 3010560 | tf_op jit(solution)/shard_map/all_gather | solution.py:168
  320.7 26.3 %copy-start.58 = (bf16[2,384,384]{2,1,0:T(8,128)(2,1)S(1)}, bf16[2,384,384]{2,1,0:T(8,128)(2,1)}, u32[]{:S(2)}) copy-start(bf16[2,384,384]{2,1,0:T(8,128)(2,1)} %param.23) | copy-start | bytes 1769476
  322.5 51.1 %all-gather.17.cloned.1.call-start = ((), (), s32[]{:S(2)}) async-start(), calls=%async_computation.16 | async-start | bytes 3010560 | tf_op jit(solution)/shard_map/all_gather | solution.py:171
  324.5 95.5 %reduce-scatter.17.cloned.1.call-start = ((), (), s32[]{:S(2)}) async-start(), calls=%async_computation.17 | async-start | bytes 3010560 | tf_op jit(solution)/shard_map/reduce_scatter | solution.py:182
  347.0 26.6 %copy-start.63 = (bf16[2,384,384]{2,1,0:T(8,128)(2,1)S(1)}, bf16[2,384,384]{2,1,0:T(8,128)(2,1)}, u32[]{:S(2)}) copy-start(bf16[2,384,384]{2,1,0:T(8,128)(2,1)} %param.25) | copy-start | bytes 1769476
  386.5 69.3 %reduce-scatter.15.cloned.1.call-start = ((), (), s32[]{:S(2)}) async-start(), calls=%async_computation.15 | async-start | bytes 3010560 | tf_op jit(solution)/shard_map/reduce_scatter | solution.py:174
  391.2 28.8 %copy-start.9 = (f32[784,384]{1,0:T(8,128)S(1)}, f32[784,384]{1,0:T(8,128)}, u32[]{:S(2)}) copy-start(f32[784,384]{1,0:T(8,128)} %copy-done.8) | copy-start | bytes 3612676
  391.2 64.6 %copy-start.90 = (f32[384]{0:T(512)S(1)}, f32[384]{0:T(512)}, u32[]{:S(2)}) copy-start(f32[384]{0:T(512)} %get-tuple-element.84) | copy-start | bytes 4612
  391.3 92.2 %all-gather.19.cloned.1.call-start = ((), (), s32[]{:S(2)}) async-start(), calls=%async_computation.18 | async-start | bytes 3010560 | tf_op jit(solution)/shard_map/all_gather | solution.py:171
  459.0 167.0 %reduce-scatter.19.cloned.1.call-start = ((), (), s32[]{:S(2)}) async-start(), calls=%async_computation.19 | async-start | bytes 3010560 | tf_op jit(solution)/shard_map/reduce_scatter | solution.py:182
  495.1 10.8 %slice-start = ((s8[5505024]{0:T(1024)(128)(4,1)}), s8[1310720]{0:T(1024)(128)(4,1)S(1)}, s32[]{:S(2)}) async-start(s8[5505024]{0:T(1024)(128)(4,1)} %bitcast.249), calls=%async_computation.25 | async-start | bytes 2621440
  500.8 5.2 slice-start.1
  500.8 5.2 copy-start.17
  500.8 5.2 copy-start.34
  581.9 6.0 copy-start.69
  592.5 33.5 %copy-start.7 = (f32[784,384]{1,0:T(8,128)S(1)}, f32[784,384]{1,0:T(8,128)}, u32[]{:S(2)}) copy-start(f32[784,384]{1,0:T(8,128)} %copy-done.5) | copy-start | bytes 3612676
  592.5 63.4 %all-gather.21.cloned.1.call-start = ((), (), s32[]{:S(2)}) async-start(), calls=%async_computation.20 | async-start | bytes 3010560 | tf_op jit(solution)/shard_map/all_gather | solution.py:171
  628.4 27.4 %copy-start.64 = (bf16[2,384,384]{2,1,0:T(8,128)(2,1)S(1)}, bf16[2,384,384]{2,1,0:T(8,128)(2,1)}, u32[]{:S(2)}) copy-start(bf16[2,384,384]{2,1,0:T(8,128)(2,1)} %param.25) | copy-start | bytes 1769476
  631.4 70.4 %reduce-scatter.21.cloned.1.call-start = ((), (), s32[]{:S(2)}) async-start(), calls=%async_computation.21 | async-start | bytes 3010560 | tf_op jit(solution)/shard_map/reduce_scatter | solution.py:182
  655.9 9.3 copy-start.59
  668.2 33.6 %copy-start.78 = (f32[784]{0:T(1024)S(1)}, f32[784]{0:T(1024)}, u32[]{:S(2)}) copy-start(f32[784]{0:T(1024)} %copy-done.77) | copy-start | bytes 9412
  668.2 33.6 %copy-start.82 = (f32[784]{0:T(1024)S(1)}, f32[784]{0:T(1024)}, u32[]{:S(2)}) copy-start(f32[784]{0:T(1024)} %copy-done.81) | copy-start | bytes 9412
  668.2 33.6 %copy-start.86 = (f32[384]{0:T(512)S(1)}, f32[384]{0:T(512)}, u32[]{:S(2)}) copy-start(f32[384]{0:T(512)} %copy-done.85) | copy-start | bytes 4612
  668.2 35.3 %copy-start.42 = (f32[784,384]{1,0:T(8,128)S(1)}, f32[784,384]{1,0:T(8,128)}, u32[]{:S(2)}) copy-start(f32[784,384]{1,0:T(8,128)} %get-tuple-element.118) | copy-start | bytes 3612676
  668.2 62.7 %all-gather.23.cloned.1.call-start = ((), (), s32[]{:S(2)}) async-start(), calls=%async_computation.22 | async-start | bytes 3010560 | tf_op jit(solution)/shard_map/all_gather | solution.py:171
  703.6 27.4 %copy-start.61 = (bf16[2,96,384]{2,1,0:T(8,128)(2,1)S(1)}, bf16[2,96,384]{2,1,0:T(8,128)(2,1)}, u32[]{:S(2)}) copy-start(bf16[2,96,384]{2,1,0:T(8,128)(2,1)} %param.22) | copy-start | bytes 442372
  706.4 169.9 %reduce-scatter.23.cloned.1.call-start = ((), (), s32[]{:S(2)}) async-start(), calls=%async_computation.23 | async-start | bytes 3010560 | tf_op jit(solution)/shard_map/reduce_scatter | solution.py:182
  733.5 9.5 slice-start.2
  770.8 179.5 %all-reduce.5.cloned.1.call-start = ((), (), s32[]{:S(2)}) async-start(), calls=%async_computation.24 | async-start | bytes 7077888 | tf_op jit(solution)/shard_map/psum | solution.py:369
  791.9 36.5 %copy-start.71 = (f32[3,49,49]{1,2,0:T(8,128)S(1)}, f32[3,49,49]{1,2,0:T(8,128)}, u32[]{:S(2)}) copy-start(f32[3,49,49]{1,2,0:T(8,128)} %get-tuple-element.126) | copy-start | bytes 86440
  793.1 41.0 %copy-start.97 = (f32[384]{0:T(512)S(1)}, f32[384]{0:T(512)}, u32[]{:S(2)}) copy-start(f32[384]{0:T(512)} %get-tuple-element.72) | copy-start | bytes 4612
  828.4 47.9 %copy-start.4 = (f32[784,384]{1,0:T(8,128)S(1)}, f32[784,384]{1,0:T(8,128)}, u32[]{:S(2)}) copy-start(f32[784,384]{1,0:T(8,128)} %param.16) | copy-start | bytes 3612676
  828.4 47.9 %copy-start.76 = (f32[784]{0:T(1024)S(1)}, f32[784]{0:T(1024)}, u32[]{:S(2)}) copy-start(f32[784]{0:T(1024)} %copy-done.75) | copy-start | bytes 9412
  828.4 47.9 %copy-start.80 = (f32[784]{0:T(1024)S(1)}, f32[784]{0:T(1024)}, u32[]{:S(2)}) copy-start(f32[784]{0:T(1024)} %copy-done.79) | copy-start | bytes 9412
  828.4 47.9 %copy-start.84 = (f32[384]{0:T(512)S(1)}, f32[384]{0:T(512)}, u32[]{:S(2)}) copy-start(f32[384]{0:T(512)} %copy-done.83) | copy-start | bytes 4612
  834.1 81.9 %copy-start.40 = (f32[784,384]{1,0:T(8,128)S(1)}, f32[784,384]{1,0:T(8,128)}, u32[]{:S(2)}) copy-start(f32[784,384]{1,0:T(8,128)} %get-tuple-element.115) | copy-start | bytes 3612676
  950.3 5.0 copy-start.54
  (73 other events, 194.0 us)
Sparse Core Ops, SparseCore 0:
  12.5 27.0 all-gather.8
  79.8 33.3 reduce-scatter.8
  116.2 24.3 all-gather.10
  160.4 33.3 reduce-scatter.10
  197.4 24.3 all-gather.12
  285.6 33.3 reduce-scatter.12
  322.6 24.3 all-gather.14
  349.2 24.3 all-gather.16
  386.6 33.3 reduce-scatter.16
  422.4 33.3 reduce-scatter.14
  459.1 24.3 all-gather.18
  592.6 33.3 reduce-scatter.18
  631.5 24.3 all-gather.20
  668.3 33.3 reduce-scatter.20
  706.6 24.3 all-gather.22
  770.9 33.3 reduce-scatter.22
  809.2 140.9 all-reduce.4
where the time goes:
time: 970 us; the launch traced here: 963 us
  waiting for transfers between devices  432 us (45%)
  local copies, waits for them, and re-layouts  204 us (21%)
  matrix products  148 us (15%)
  other arithmetic  85.8 us (9%)
  blocking collectives  76.6 us (8%)
  between operations  16.2 us (2%)
    reduce_scatter x4, waiting for transfers between devices, branch_total(): lax.psum_scatter(product(jnp.int32(0), lax.axis_size('head') * own_rows)....  134 us
    reduce_scatter x4, waiting for transfers between devices, input_total(): lax.psum_scatter(product(jnp.int32(0), lax.axis_size('head') * own_rows)....  95.6 us
    all_gather x4, waiting for transfers between devices, norm_rows(): return lax.all_gather(values, 'head', axis=0, tiled=True)  87.5 us
    all_gather x4, waiting for transfers between devices, grad_rows(): return lax.all_gather(values, 'head', axis=0, tiled=True)  83 us
    psum x1, blocking collectives, body(): lax.psum((qkv_total, qv_total, table_total, proj_total, fc1_total, fc1_bi...  38.7 us
    psum x1, blocking collectives, body(): lax.psum((jnp.stack(gain_list), jnp.stack(shift_list)), ('dp', 'head'))  37.8 us
    slice x1, local copies, waits for them, and re-layouts, body(): qv_grad = jnp.sum(stacked[:, 0::2].astype(wide_type), axis=0)  35.3 us
    psum x1, waiting for transfers between devices, body(): lax.psum((qkv_total, qv_total, table_total, proj_total, fc1_total, fc1_bi...  31.6 us
  transfers between devices with their start and end apart: 17, of which 16 were waited for; matrix products, arithmetic and copies ran while one was open for 11% of the time, Pallas kernels for 0%

commit v1 on v0

v1 whole, which is shorter than its diff:
```python
import jax
import jax.numpy as jnp
import numpy as np
from jax import lax
from jax.experimental import pallas as pl
from jax.experimental.pallas import tpu as pltpu
from jax.sharding import PartitionSpec as P

D = 384
FF = 1536
LAYERS = 2
PLACES = 49
PAD = 56
WIDE = 64
QUADS = 3
HEAD_DIM = 32
SCORE_SCALE = HEAD_DIM**-0.5
LN_EPS = 1e-05
LOW = jnp.bfloat16
F32 = jnp.float32
VMEM_BYTES = 56 * 1024 * 1024

SRC, SIDE, WROW, WCOL, FIRST, RET, SEND = 0, 24, 48, 72, 96, 120, 140
TABLE = 144


def vmem():
    return pl.BlockSpec(memory_space=pltpu.VMEM)


def smem():
    return pl.BlockSpec(memory_space=pltpu.SMEM)


def params(limit=VMEM_BYTES):
    return pltpu.CompilerParams(vmem_limit_bytes=limit)


def cost(flops, size):
    return pl.CostEstimate(flops=int(flops), bytes_accessed=int(size), transcendentals=0)


def dot_nn(a, b):
    return lax.dot_general(a, b, (((1,), (0,)), ((), ())), preferred_element_type=F32)


def dot_nt(a, b):
    return lax.dot_general(a, b, (((1,), (1,)), ((), ())), preferred_element_type=F32)


def dot_tn(a, b):
    return lax.dot_general(a, b, (((0,), (0,)), ((), ())), preferred_element_type=F32)


def plan_kernel(own, bins, kind_ref, me_ref, out_ref, load_ref):
    me = me_ref[0]
    half = 2 * own
    for i in range(TABLE):
        out_ref[i] = -1 if i < bins or RET <= i < RET + own else 0
    for i in range(bins):
        out_ref[SIDE + i] = 1
        out_ref[FIRST + i] = i
    for i in range(4):
        load_ref[i] = 0

    def place(start, count, side, bin_id):
        base = load_ref[bin_id]
        load_ref[bin_id] = base + count

        def step(k, carry):
            slot = start + k
            owner = slot // own
            inner = slot - owner * own
            local = base + k
            mine = bin_id == me
            halo = jnp.where(me == 1, slot - half, slot - half + 4)
            code = jnp.where(
                owner == me, inner, jnp.where(owner == (me ^ 1), own + inner, 2 * own + halo)
            )

            @pl.when(mine)
            def _():
                wrow = k // side
                out_ref[SRC + local] = code
                out_ref[SIDE + local] = side
                out_ref[WROW + local] = wrow
                out_ref[WCOL + local] = k - wrow * side
                out_ref[FIRST + local] = base

            @pl.when(owner == me)
            def _():
                back = jnp.where(me == 2, slot - half, k)
                out_ref[RET + inner] = jnp.where(
                    mine, local, jnp.where(bin_id == (me ^ 1), bins + local, 2 * bins + back)
                )

            return carry

        lax.fori_loop(0, count, step, 0)

    for turn in range(3):

        def visit(i, start, turn=turn):
            kind = kind_ref[0, i]
            count = jnp.where(kind == 2, 9, jnp.where(kind == 1, 4, 0))
            side = jnp.where(kind == 2, 3, 2)
            cut = half - start
            across = (cut > 0) & (cut < count)
            second = (start >= half) | (across & (cut < count - cut))
            chip = jnp.where(second, 1, 0)
            left, right = load_ref[2 * chip], load_ref[2 * chip + 1]
            emptier = 2 * chip + jnp.where(left <= right, 0, 1)
            if turn == 0:
                chosen, bin_id = across, 1 + chip
            else:
                chosen, bin_id = (kind == 3 - turn) & jnp.logical_not(across), emptier

            @pl.when(chosen)
            def _():
                place(start, count, side, bin_id)
                if turn == 0:
                    out_ref[SEND] = jnp.where((me == 1) & (chip == 0), cut, 0)

            return start + count

        lax.fori_loop(0, kind_ref.shape[1], visit, jnp.int32(0))


def make_plan(image_kind, me, own, bins):
    def kernel(kind_ref, me_ref, out_ref, load_ref):
        plan_kernel(own, bins, kind_ref, me_ref, out_ref, load_ref)

    return pl.pallas_call(
        kernel,
        out_shape=jax.ShapeDtypeStruct((TABLE,), jnp.int32),
        in_specs=[smem(), smem()],
        out_specs=smem(),
        scratch_shapes=[pltpu.SMEM((4,), jnp.int32)],
        name="plan",
    )(image_kind, me.reshape(1))


def gather_slots(table, mine, partner, halo, bins):
    own = mine.shape[0] // PLACES

    def kernel(table_ref, mine_ref, partner_ref, halo_ref, out_ref, spread_ref):
        spread_ref[...] = jnp.zeros(spread_ref.shape, F32)
        at = 0
        for ref in (mine_ref, partner_ref, halo_ref):
            for s in range(ref.shape[0] // PLACES):
                spread_ref[at, 0:PLACES] = ref[s * PLACES : (s + 1) * PLACES].astype(F32)
                at += 1

        def step(j, carry):
            src = table_ref[SRC + j]

            @pl.when(src < 0)
            def _():
                out_ref[j] = jnp.zeros((PAD, D), F32)

            @pl.when(src >= 0)
            def _():
                out_ref[j] = spread_ref[src]

            return carry

        lax.fori_loop(0, bins, step, 0)

    out = pl.pallas_call(
        kernel,
        out_shape=jax.ShapeDtypeStruct((bins, PAD, D), F32),
        in_specs=[smem(), vmem(), vmem(), vmem()],
        out_specs=vmem(),
        scratch_shapes=[pltpu.VMEM((2 * own + 4, PAD, D), F32)],
        compiler_params=params(),
        cost_estimate=cost(0, 5e6),
        name="gather_slots",
    )(table, mine, partner, halo)
    return out.reshape(bins * PAD, D)


def return_slots(table, mine, partner, halo, own):
    bins = mine.shape[0]

    def kernel(table_ref, mine_ref, partner_ref, halo_ref, out_ref):
        for s in range(own):
            src = table_ref[RET + s]
            rows = pl.ds(s * PLACES, PLACES)

            @pl.when(src < 0)
            def _():
                out_ref[rows] = jnp.zeros((PLACES, D), F32)

            @pl.when((src >= 0) & (src < bins))
            def _():
                out_ref[rows] = mine_ref[src, 0:PLACES]

            @pl.when((src >= bins) & (src < 2 * bins))
            def _():
                out_ref[rows] = partner_ref[src - bins, 0:PLACES]

            @pl.when(src >= 2 * bins)
            def _():
                out_ref[rows] = halo_ref[src - 2 * bins, 0:PLACES]

    return pl.pallas_call(
        kernel,
        out_shape=jax.ShapeDtypeStruct((own * PLACES, D), F32),
        in_specs=[smem(), vmem(), vmem(), vmem()],
        out_specs=vmem(),
        compiler_params=params(),
        cost_estimate=cost(0, 5e6),
        name="return_slots",
    )(table, mine, partner, halo)


def norm_rows(rows):
    average = jnp.mean(rows, axis=-1, keepdims=True)
    centred = rows - average
    inverse = lax.rsqrt(jnp.mean(centred * centred, axis=-1, keepdims=True) + LN_EPS)
    return centred * inverse, inverse


def norm_back(incoming, scaled, inverse, gain):
    weighted = incoming * gain
    return inverse * (
        weighted
        - jnp.mean(weighted, axis=-1, keepdims=True)
        - scaled * jnp.mean(weighted * scaled, axis=-1, keepdims=True)
    )


def gelu_parts(x):
    size = jnp.abs(x) * 0.7071067811865476
    t = 1.0 / (1.0 + 0.3275911 * size)
    bell = jnp.exp(-0.5 * x * x)
    poly = t * (
        0.127414796 + t * (-0.142248368 + t * (0.7107068705 + t * (-0.7265760135 + t * 0.5307027145)))
    )
    tail = poly * bell
    phi = jnp.where(x >= 0, 1.0 - tail, tail)
    return x * phi, phi + x * bell * 0.3989422804014327


def place_parts(shape, dim):
    place = lax.broadcasted_iota(jnp.int32, shape, dim)
    row = (place * 37) >> 8
    return place, row, place - 7 * row


def fill_moves(table_ref, out_ref, bins, back):
    width = out_ref.shape[1]
    place, row, col = place_parts((PAD, 1), 0)
    if back:
        row_other, col_other = row < 3, col < 3
        inner = 7 * jnp.where(row_other, row + 4, row - 3) + jnp.where(col_other, col + 4, col - 3)
    else:
        row_other, col_other = row >= 4, col >= 4
        inner = 7 * jnp.where(row_other, row - 4, row + 3) + jnp.where(col_other, col - 4, col + 3)
    lanes = lax.broadcasted_iota(jnp.int32, (2 * PAD, width), 1)

    def source(w):
        side, wrow, wcol = table_ref[SIDE + w], table_ref[WROW + w], table_ref[WCOL + w]
        first = table_ref[FIRST + w]
        if back:
            orow = jnp.where(wrow == 0, side - 1, wrow - 1)
            ocol = jnp.where(wcol == 0, side - 1, wcol - 1)
        else:
            orow = jnp.where(wrow == side - 1, 0, wrow + 1)
            ocol = jnp.where(wcol == side - 1, 0, wcol + 1)
        slot = first + jnp.where(row_other, orow, wrow) * side + jnp.where(col_other, ocol, wcol)
        return jnp.where(place < PLACES, slot * PAD + inner, w * PAD + place)

    def step(j, carry):
        rows = jnp.concatenate([source(2 * j), source(2 * j + 1)], axis=0)
        hot = jnp.where(lanes == rows, 1.0, 0.0).astype(LOW)
        out_ref[pl.ds(pl.multiple_of(j * 2 * PAD, 16), 2 * PAD)] = hot
        return carry

    lax.fori_loop(0, bins // 2, step, 0)


def head_marks():
    lane = lax.broadcasted_iota(jnp.int32, (WIDE, 128), 1) // HEAD_DIM
    return [jnp.where(lane == h, 1.0, 0.0).astype(LOW) for h in range(4)]


def spread(block, marks):
    return jnp.concatenate([block * mark for mark in marks], axis=0)


def fold(product, marks):
    total = None
    for h, mark in enumerate(marks):
        part = product[h * WIDE : (h + 1) * WIDE] * mark.astype(F32)
        total = part if total is None else total + part
    return total


def by_segment(values, reduce, neutral):
    lane = lax.broadcasted_iota(jnp.int32, (values.shape[0], 128), 1) < WIDE
    parts = []
    for half in range(2):
        part = values[:, half * 128 : (half + 1) * 128]
        left = reduce(jnp.where(lane, part, neutral), axis=-1, keepdims=True)
        right = reduce(jnp.where(lane, neutral, part), axis=-1, keepdims=True)
        parts.append(jnp.where(lane, left, right))
    return jnp.concatenate(parts, axis=1)


def pad_rows(rows):
    return jnp.concatenate([rows, jnp.zeros((WIDE - PAD, rows.shape[1]), rows.dtype)], axis=0)


def stack_qkv(pieces, out_ref):
    for k, piece in enumerate(pieces):
        for c in range(3):
            out_ref[c * D + k * 96 : c * D + (k + 1) * 96] = piece[c * 96 : (c + 1) * 96]


def stack_proj(pieces, out_ref):
    for k, piece in enumerate(pieces):
        out_ref[k * 96 : (k + 1) * 96] = piece[288:384]


def stack_mlp(pieces, fc1_ref, fc2_ref):
    for k, piece in enumerate(pieces):
        fc1_ref[:, k * D : (k + 1) * D] = piece[0:D]
        fc2_ref[k * D : (k + 1) * D] = piece[D : 2 * D]


def attn_forward(table, hidden, weights, qv_bias, bias, norms, shifted):
    rows = hidden.shape[0]
    bins = rows // PAD
    chunk_slots = 6
    chunk = chunk_slots * PAD
    wide_rows = -(-rows // 128) * 128

    def kernel(
        table_ref, hidden_ref, w0, w1, w2, w3, qv_ref, bias_ref, norm_ref,
        mid_ref, a_ref, qkv_ref, p_ref, attn_ref,
        wqkv, wproj, wide_attn, moves,
    ):
        pieces = (w0, w1, w2, w3)
        stack_qkv(pieces, wqkv)
        stack_proj(pieces, wproj)
        gain, shift, proj_shift = norm_ref[0:1], norm_ref[1:2], norm_ref[2:3]
        marks = head_marks()
        dest = attn_ref if shifted else a_ref

        def norm_step(i, carry):
            at = pl.ds(pl.multiple_of(i * chunk, 16), chunk)
            scaled, _ = norm_rows(hidden_ref[at])
            dest[at] = (scaled * gain + shift).astype(LOW)
            return carry

        lax.fori_loop(0, bins // chunk_slots, norm_step, 0)
        if shifted:
            fill_moves(table_ref, moves, bins, False)
            a_ref[...] = dot_nn(moves[:, 0:rows], dest[...]).astype(LOW)
            fill_moves(table_ref, moves, bins, True)

        def qkv_step(i, carry):
            at = pl.ds(pl.multiple_of(i * chunk, 16), chunk)
            project = dot_nt(a_ref[at], wqkv[...]) + qv_ref[...]
            for j in range(chunk_slots):
                block = project[j * PAD : (j + 1) * PAD]
                qkv_ref[i * chunk_slots + j] = pad_rows(block).astype(LOW)
            return carry

        lax.fori_loop(0, bins // chunk_slots, qkv_step, 0)

        if shifted:
            _, prow, pcol = place_parts((PAD, 1), 0)
            lane = lax.broadcasted_iota(jnp.int32, (1, 4 * WIDE), 1)
            qplace = lane - (lane >> 6) * WIDE
            qrow = (qplace * 37) >> 8
            qcol = qplace - 7 * qrow
            pband = 1 + (prow >= 4).astype(jnp.int32), 1 + (pcol >= 4).astype(jnp.int32)
            qband = 1 + (qrow >= 4).astype(jnp.int32), 1 + (qcol >= 4).astype(jnp.int32)

        def window(w, carry):
            if shifted:
                side = table_ref[SIDE + w]
                low_row = jnp.where(table_ref[WROW + w] == side - 1, 3, 0)
                low_col = jnp.where(table_ref[WCOL + w] == side - 1, 1, 0)
                pregion = low_row * pband[0] + low_col * pband[1]
                qregion = low_row * qband[0] + low_col * qband[1]
                mask = jnp.where(pregion != qregion, -100.0, 0.0)
            for t in range(QUADS):
                cols = slice(t * 128, (t + 1) * 128)
                q = qkv_ref[w, :, t * 128 : (t + 1) * 128]
                k = qkv_ref[w, :, D + t * 128 : D + (t + 1) * 128]
                v = qkv_ref[w, :, 2 * D + t * 128 : 2 * D + (t + 1) * 128]
                scores = dot_nt(q, spread(k, marks))[0:PAD] * SCORE_SCALE + bias_ref[t]
                if shifted:
                    scores = scores + mask
                exponent = jnp.exp(scores - by_segment(scores, jnp.max, -3e38))
                total = by_segment(exponent, jnp.sum, 0.0)
                probs = pad_rows(exponent / total).astype(LOW)
                p_ref[w, t] = probs
                at = pl.ds(pl.multiple_of(w * PAD, 8), PAD)
                wide_attn[at, cols] = dot_nn(probs, spread(v, marks))[0:PAD]
            return carry

        lax.fori_loop(0, bins, window, 0)
        if shifted:
            attn_ref[...] = dot_nn(moves[:, 0:rows], wide_attn[...].astype(LOW)).astype(LOW)
        else:
            attn_ref[...] = wide_attn[...].astype(LOW)

        def proj_step(i, carry):
            at = pl.ds(pl.multiple_of(i * chunk, 16), chunk)
            mid_ref[at] = hidden_ref[at] + dot_nn(attn_ref[at], wproj[...]) + proj_shift
            return carry

        lax.fori_loop(0, bins // chunk_slots, proj_step, 0)

    return pl.pallas_call(
        kernel,
        out_shape=(
            jax.ShapeDtypeStruct((rows, D), F32),
            jax.ShapeDtypeStruct((rows, D), LOW),
            jax.ShapeDtypeStruct((bins, WIDE, 3 * D), LOW),
            jax.ShapeDtypeStruct((bins, QUADS, WIDE, 4 * WIDE), LOW),
            jax.ShapeDtypeStruct((rows, D), LOW),
        ),
        in_specs=[smem()] + [vmem()] * 8,
        out_specs=[vmem()] * 5,
        scratch_shapes=[
            pltpu.VMEM((3 * D, D), LOW),
            pltpu.VMEM((D, D), LOW),
            pltpu.VMEM((rows, D), F32),
            pltpu.VMEM((rows if shifted else 16, wide_rows), LOW),
        ],
        compiler_params=params(),
        cost_estimate=cost(8e9, 1.2e7),
        name="attn_forward",
    )(table, hidden, *weights, qv_bias, bias, norms)


def attn_backward(table, grad, hidden, a, qkv, probs, attn, weights, norms, shifted):
    rows = hidden.shape[0]
    bins = rows // PAD
    chunk_slots = 6
    chunk = chunk_slots * PAD
    wide_rows = -(-rows // 128) * 128

    def kernel(
        table_ref, grad_ref, hidden_ref, a_ref, qkv_ref, p_ref, attn_ref, w0, w1, w2, w3, norm_ref,
        out_ref, keep_ref, send_ref, small_ref, bias_ref,
        wqkv, wproj, low_grad, wide_attn, low_wide, gqkv, moves,
    ):
        pieces = (w0, w1, w2, w3)
        stack_qkv(pieces, wqkv)
        stack_proj(pieces, wproj)
        gain = norm_ref[0:1]
        marks = head_marks()
        steps = bins // chunk_slots
        if shifted:
            fill_moves(table_ref, moves, bins, False)

        def proj_step(i, total):
            at = pl.ds(pl.multiple_of(i * chunk, 16), chunk)
            gz = grad_ref[at].astype(LOW)
            low_grad[at] = gz
            gattn = dot_nt(gz, wproj[...])
            if shifted:
                low_wide[at] = gattn.astype(LOW)
            else:
                for j in range(chunk_slots):
                    block = gattn[j * PAD : (j + 1) * PAD]
                    wide_attn[i * chunk_slots + j] = pad_rows(block).astype(LOW)
            return total + jnp.sum(gz.astype(F32), axis=0, keepdims=True)

        proj_shift = lax.fori_loop(0, steps, proj_step, jnp.zeros((1, D), F32))
        if shifted:

            def move_step(i, carry):
                at = pl.ds(pl.multiple_of(i * chunk, 16), chunk)
                moved = dot_nn(moves[at, 0:rows], low_wide[...])
                for j in range(chunk_slots):
                    block = moved[j * PAD : (j + 1) * PAD]
                    wide_attn[i * chunk_slots + j] = pad_rows(block).astype(LOW)
                return carry

            lax.fori_loop(0, steps, move_step, 0)
            fill_moves(table_ref, moves, bins, True)
        dproj = dot_tn(attn_ref[...], low_grad[...]).astype(LOW)
        for k in range(4):
            dest = keep_ref if k < 2 else send_ref
            dest[k % 2, 288:384] = dproj[k * 96 : (k + 1) * 96]

        bias_ref[...] = jnp.zeros((QUADS, PAD, 4 * WIDE), F32)

        def window(w, carry):
            for t in range(QUADS):
                q = qkv_ref[w, :, t * 128 : (t + 1) * 128]
                k = qkv_ref[w, :, D + t * 128 : D + (t + 1) * 128]
                v = qkv_ref[w, :, 2 * D + t * 128 : 2 * D + (t + 1) * 128]
                low_probs = p_ref[w, t]
                p = low_probs.astype(F32)
                go = wide_attn[w, :, t * 128 : (t + 1) * 128]
                gp = dot_nt(go, spread(v, marks))
                ds = p * (gp - by_segment(gp * p, jnp.sum, 0.0))
                low_ds = ds.astype(LOW)
                bias_ref[t] += low_ds.astype(F32)[0:PAD]
                gq = dot_nn(low_ds, spread(k, marks)) * SCORE_SCALE
                gk = fold(dot_tn(low_ds, q), marks) * SCORE_SCALE
                gv = fold(dot_tn(low_probs, go), marks)
                at = pl.ds(pl.multiple_of(w * PAD, 8), PAD)
                gqkv[at, t * 128 : (t + 1) * 128] = gq[0:PAD]
                gqkv[at, D + t * 128 : D + (t + 1) * 128] = gk[0:PAD]
                gqkv[at, 2 * D + t * 128 : 2 * D + (t + 1) * 128] = gv[0:PAD]
            return carry

        lax.fori_loop(0, bins, window, 0)

        low_qkv = gqkv[...].astype(LOW)
        sums = jnp.sum(low_qkv.astype(F32), axis=0, keepdims=True)
        dqkv = dot_tn(a_ref[...], low_qkv)
        for c in range(3):
            turned = dqkv[:, c * D : (c + 1) * D].T.astype(LOW)
            for k in range(4):
                dest = keep_ref if k < 2 else send_ref
                dest[k % 2, c * 96 : (c + 1) * 96] = turned[k * 96 : (k + 1) * 96]
        if shifted:
            low_wide[...] = dot_nn(low_qkv, wqkv[...]).astype(LOW)

        def back_step(i, totals):
            at = pl.ds(pl.multiple_of(i * chunk, 16), chunk)
            if shifted:
                ga = dot_nn(moves[at, 0:rows], low_wide[...])
            else:
                ga = dot_nn(gqkv[at].astype(LOW), wqkv[...])
            scaled, inverse = norm_rows(hidden_ref[at])
            out_ref[at] = grad_ref[at] + norm_back(ga, scaled, inverse, gain)
            return (
                totals[0] + jnp.sum(ga * scaled, axis=0, keepdims=True),
                totals[1] + jnp.sum(ga, axis=0, keepdims=True),
            )

        zero = jnp.zeros((1, D), F32)
        dgain, dshift = lax.fori_loop(0, steps, back_step, (zero, zero))
        small_ref[0:1] = dgain
        small_ref[1:2] = dshift
        small_ref[2:3] = proj_shift
        small_ref[3:4] = sums[:, 0:D]
        small_ref[4:5] = sums[:, 2 * D : 3 * D]
        small_ref[5:8] = jnp.zeros((3, D), F32)

    return pl.pallas_call(
        kernel,
        out_shape=(
            jax.ShapeDtypeStruct((rows, D), F32),
            jax.ShapeDtypeStruct((2, D, D), LOW),
            jax.ShapeDtypeStruct((2, D, D), LOW),
            jax.ShapeDtypeStruct((8, D), F32),
            jax.ShapeDtypeStruct((QUADS, PAD, 4 * WIDE), F32),
        ),
        in_specs=[smem()] + [vmem()] * 11,
        out_specs=[vmem()] * 5,
        scratch_shapes=[
            pltpu.VMEM((3 * D, D), LOW),
            pltpu.VMEM((D, D), LOW),
            pltpu.VMEM((rows, D), LOW),
            pltpu.VMEM((bins, WIDE, D), LOW),
            pltpu.VMEM((rows, D), LOW),
            pltpu.VMEM((rows, 3 * D), F32),
            pltpu.VMEM((rows if shifted else 16, wide_rows), LOW),
        ],
        compiler_params=params(),
        cost_estimate=cost(1.6e10, 1.2e7),
        name="attn_backward",
    )(table, grad, hidden, a, qkv, probs, attn, *weights, norms)


def mlp_forward(mid, weights, fc1_bias, norms):
    rows = mid.shape[0]
    chunk = 3 * PAD * 2
    steps = rows // chunk

    def kernel(
        mid_ref, w0, w1, w2, w3, fc1_bias_ref, norm_ref,
        out_ref, a_ref, act_ref, slope_ref, fc1, fc2,
    ):
        stack_mlp((w0, w1, w2, w3), fc1, fc2)
        gain, shift, out_shift = norm_ref[0:1], norm_ref[1:2], norm_ref[2:3]

        def step(i, carry):
            at = pl.ds(pl.multiple_of(i * chunk, 16), chunk)
            rows_now = mid_ref[at]
            scaled, _ = norm_rows(rows_now)
            a = (scaled * gain + shift).astype(LOW)
            a_ref[at] = a
            act, slope = gelu_parts(dot_nn(a, fc1[...]) + fc1_bias_ref[...])
            act = act.astype(LOW)
            act_ref[at] = act
            slope_ref[at] = slope.astype(LOW)
            out_ref[at] = rows_now + dot_nn(act, fc2[...]) + out_shift
            return carry

        lax.fori_loop(0, steps, step, 0)

    return pl.pallas_call(
        kernel,
        out_shape=(
            jax.ShapeDtypeStruct((rows, D), F32),
            jax.ShapeDtypeStruct((rows, D), LOW),
            jax.ShapeDtypeStruct((rows, FF), LOW),
            jax.ShapeDtypeStruct((rows, FF), LOW),
        ),
        in_specs=[vmem()] * 7,
        out_specs=[vmem()] * 4,
        scratch_shapes=[pltpu.VMEM((D, FF), LOW), pltpu.VMEM((FF, D), LOW)],
        compiler_params=params(),
        cost_estimate=cost(8e9, 1.2e7),
        name="mlp_forward",
    )(mid, *weights, fc1_bias, norms)


def mlp_backward(grad, mid, a, act, slope, weights, norms):
    rows = mid.shape[0]
    chunk = 3 * PAD * 2
    steps = rows // chunk

    def kernel(
        grad_ref, mid_ref, a_ref, act_ref, slope_ref, w0, w1, w2, w3, norm_ref,
        out_ref, keep_ref, send_ref, small_ref, bias_ref, fc1, fc2, low_grad, gpre_ref,
    ):
        stack_mlp((w0, w1, w2, w3), fc1, fc2)
        gain = norm_ref[0:1]

        def step(i, totals):
            at = pl.ds(pl.multiple_of(i * chunk, 16), chunk)
            grad_now = grad_ref[at]
            gz = grad_now.astype(LOW)
            low_grad[at] = gz
            gpre = (dot_nt(gz, fc2[...]) * slope_ref[at].astype(F32)).astype(LOW)
            gpre_ref[at] = gpre
            ga = dot_nt(gpre, fc1[...])
            scaled, inverse = norm_rows(mid_ref[at])
            out_ref[at] = grad_now + norm_back(ga, scaled, inverse, gain)
            return (
                totals[0] + jnp.sum(ga * scaled, axis=0, keepdims=True),
                totals[1] + jnp.sum(ga, axis=0, keepdims=True),
                totals[2] + jnp.sum(gz.astype(F32), axis=0, keepdims=True),
                totals[3] + jnp.sum(gpre.astype(F32), axis=0, keepdims=True),
            )

        zero = jnp.zeros((1, D), F32)
        sums = lax.fori_loop(0, steps, step, (zero, zero, zero, jnp.zeros((1, FF), F32)))
        for i in range(3):
            small_ref[i : i + 1] = sums[i]
        small_ref[3:8] = jnp.zeros((5, D), F32)
        bias_ref[...] = sums[3]
        for k in range(4):
            dest = keep_ref if k < 2 else send_ref
            cols = slice(k * D, (k + 1) * D)
            dest[k % 2, 0:D] = dot_tn(a_ref[...], gpre_ref[:, cols]).astype(LOW)
            dest[k % 2, D : 2 * D] = dot_tn(low_grad[...], act_ref[:, cols]).astype(LOW)

    return pl.pallas_call(
        kernel,
        out_shape=(
            jax.ShapeDtypeStruct((rows, D), F32),
            jax.ShapeDtypeStruct((2, 2 * D, D), LOW),
            jax.ShapeDtypeStruct((2, 2 * D, D), LOW),
            jax.ShapeDtypeStruct((8, D), F32),
            jax.ShapeDtypeStruct((1, FF), F32),
        ),
        in_specs=[vmem()] * 10,
        out_specs=[vmem()] * 5,
        scratch_shapes=[
            pltpu.VMEM((D, FF), LOW),
            pltpu.VMEM((FF, D), LOW),
            pltpu.VMEM((rows, D), LOW),
            pltpu.VMEM((rows, FF), LOW),
        ],
        compiler_params=params(),
        cost_estimate=cost(1.6e10, 1.5e7),
        name="mlp_backward",
    )(grad, mid, a, act, slope, *weights, norms)


def swap_core(value):
    return lax.ppermute(value, "head", [(i, i ^ 1) for i in range(4)])


def swap_chip(value):
    return lax.ppermute(value, "head", [(i, i ^ 2) for i in range(4)])


def swap_border(value):
    return lax.ppermute(value, "head", [(1, 2), (2, 1)])


def swap_dp(value, step, size):
    return lax.ppermute(value, "dp", [(i, i ^ step) for i in range(size)])


def sum_head(keep, send):
    halves = keep.astype(F32) + swap_core(send).astype(F32)
    other = swap_chip(halves[1].astype(send.dtype))
    return halves[0] + other.astype(F32)


def sum_dp(value, low):
    size = lax.axis_size("dp")
    me = lax.axis_index("dp")
    bits = [1 << b for b in range(size.bit_length() - 1)]
    for bit in bits:
        mine = (me // bit) % 2
        half = value.shape[0] // 2
        sent = lax.dynamic_slice_in_dim(value, (1 - mine) * half, half, 0).astype(low)
        kept = lax.dynamic_slice_in_dim(value, mine * half, half, 0)
        value = kept + swap_dp(sent, bit, size).astype(F32)
    value = value.astype(low)
    for bit in reversed(bits):
        mine = (me // bit) % 2
        other = swap_dp(value, bit, size)
        value = jnp.where(
            mine == 0, jnp.concatenate([value, other]), jnp.concatenate([other, value])
        )
    return value.astype(F32)


def sum_dp_small(value):
    size = lax.axis_size("dp")
    for b in range(size.bit_length() - 1):
        value = value + swap_dp(value, 1 << b, size)
    return value


def relative_hot():
    place = np.arange(PLACES)
    row, col = place // 7, place % 7
    index = (row[:, None] - row[None, :] + 6) * 13 + col[:, None] - col[None, :] + 6
    return jnp.asarray((index.reshape(-1)[:, None] == np.arange(169)[None, :]).astype(np.float32))


def body(
    tokens, outputs_grad, image_kind, qkv_weight, qv_bias, bias_table, proj_weight,
    fc1_weight, fc1_bias, fc2_weight, gains, shifts,
):
    highest = lax.Precision.HIGHEST
    own = tokens.shape[0] // PLACES
    bins = own + 2
    me = lax.axis_index("head").astype(jnp.int32)
    table = make_plan(image_kind, me, own, bins)

    turned = jnp.transpose(qkv_weight, (0, 2, 3, 1)).reshape(LAYERS, 288, D)
    packs = []
    for l in range(LAYERS):
        packs.append(jnp.concatenate([turned[l], proj_weight[l]], axis=0))
        packs.append(jnp.concatenate([fc1_weight[l], fc2_weight[l]], axis=0))
    small = jnp.concatenate(
        [qv_bias.reshape(1, -1), fc1_bias, jnp.pad(bias_table.reshape(-1), (0, 138)).reshape(3, D)]
    )
    small_pair = jnp.stack([small, swap_chip(small)])
    smalls = jnp.concatenate([small_pair, swap_core(small_pair)])
    gathered = []
    for pack in packs:
        chip = swap_chip(pack)
        gathered.append((pack, chip, swap_core(pack), swap_core(chip)))

    qv_all = smalls[:, 0].reshape(4, LAYERS, 2, 96).transpose(1, 2, 0, 3).reshape(LAYERS, 2, D)
    qkv_bias = jnp.stack([qv_all[:, 0], jnp.zeros_like(qv_all[:, 0]), qv_all[:, 1]], axis=1)
    qkv_bias = qkv_bias.reshape(LAYERS, 1, 3 * D)
    fc1_all = smalls[:, 1:3].transpose(1, 0, 2).reshape(LAYERS, 1, FF)
    tables = smalls[:, 3:6].reshape(4, -1)[:, : LAYERS * 169 * 3].reshape(4, LAYERS, 169, 3)
    hot = relative_hot()
    looked = jnp.einsum("nt,kltj->lkjn", hot, tables, precision=highest)
    looked = looked.reshape(LAYERS, QUADS, 4, PLACES, PLACES)
    looked = jnp.pad(looked, ((0, 0),) * 4 + ((0, WIDE - PLACES),), constant_values=-1e30)
    looked = jnp.pad(looked, ((0, 0),) * 3 + ((0, PAD - PLACES), (0, 0)))
    bias = looked.transpose(0, 1, 3, 2, 4).reshape(LAYERS, QUADS, PAD, 4 * WIDE)

    def border(value):
        edge = 4 * PLACES
        return swap_border(jnp.where(me == 1, value[-edge:], value[:edge]))

    hidden = gather_slots(table, tokens, swap_core(tokens), border(tokens), bins)
    grad = gather_slots(
        table, outputs_grad, swap_core(outputs_grad), border(outputs_grad), bins
    )

    def norm_pack(l, which, bias_row):
        rows = jnp.stack([gains[l, which], shifts[l, which], shifts[l, bias_row]])
        return jnp.pad(rows, ((0, 5), (0, 0)))

    saved = []
    for l in range(LAYERS):
        norms = norm_pack(l, 0, 2)
        mid, a, qkv, probs, attn = attn_forward(
            table, hidden, gathered[2 * l], qkv_bias[l], bias[l], norms, l % 2 == 1
        )
        mlp_norms = norm_pack(l, 1, 3)
        out, a2, act, slope = mlp_forward(mid, gathered[2 * l + 1], fc1_all[l], mlp_norms)
        saved.append((hidden, mid, a, qkv, probs, attn, a2, act, slope, norms, mlp_norms))
        hidden = out

    def give_back(value):
        slots = value.reshape(bins, PAD, D)
        edge = lax.dynamic_slice_in_dim(slots, table[SEND], 4, 0)
        return return_slots(table, slots, swap_core(slots), swap_border(edge), own)

    output = give_back(hidden)

    mlp_grads, attn_grads = [None] * LAYERS, [None] * LAYERS
    keep_small, send_small = [None] * LAYERS, [None] * LAYERS
    for l in reversed(range(LAYERS)):
        hidden, mid, a, qkv, probs, attn, a2, act, slope, norms, mlp_norms = saved[l]
        grad, keep, send, small_mlp, dfc1_bias = mlp_backward(
            grad, mid, a2, act, slope, gathered[2 * l + 1], mlp_norms
        )
        mlp_grads[l] = sum_dp(sum_head(keep, send), LOW)
        grad, keep, send, small_attn, dscores = attn_backward(
            table, grad, hidden, a, qkv, probs, attn, gathered[2 * l], norms, l % 2 == 1
        )
        attn_grads[l] = sum_dp(sum_head(keep, send), LOW)
        dscores = dscores.reshape(QUADS, PAD, 4, WIDE)[:, :PLACES, :, :PLACES]
        dscores = dscores.transpose(0, 2, 1, 3).reshape(12, PLACES * PLACES)
        dtable = jnp.einsum("nt,hn->ht", hot, dscores, precision=highest).reshape(4, 3, 169)
        dtable = jnp.pad(dtable.reshape(4, 507), ((0, 0), (0, 261))).reshape(4, 2, D)
        dqv = small_attn[3:5].reshape(2, 4, 96).transpose(1, 0, 2).reshape(4, 192)
        dqv = jnp.pad(dqv, ((0, 0), (0, 192))).reshape(4, 1, D)
        shared = jnp.concatenate([small_attn[0:3], small_mlp[0:3]])
        shared = jnp.broadcast_to(shared[None], (4, 6, D))
        rows = jnp.concatenate([shared, dfc1_bias.reshape(4, 1, D), dqv, dtable], axis=1)
        keep_small[l], send_small[l] = rows[:2], rows[2:]
    tokens_grad = give_back(grad)

    total = sum_head(jnp.concatenate(keep_small, axis=1), jnp.concatenate(send_small, axis=1))
    total = sum_dp_small(total).reshape(LAYERS, 10, D)
    gains_out = jnp.stack([total[:, 0], total[:, 3]], axis=1)
    shifts_out = jnp.stack([total[:, 1], total[:, 4], total[:, 2], total[:, 5]], axis=1)
    fc1_bias_out = total[:, 6]
    qv_out = total[:, 7, :192].reshape(LAYERS, 2, 96)
    table_out = total[:, 8:10].reshape(LAYERS, 2 * D)[:, :507].reshape(LAYERS, 3, 169)
    table_out = table_out.transpose(0, 2, 1)
    attn_all = jnp.stack(attn_grads)
    qkv_out = attn_all[:, :288].reshape(LAYERS, 3, 96, D).transpose(0, 3, 1, 2)
    proj_out = attn_all[:, 288:]
    mlp_all = jnp.stack(mlp_grads)
    fc1_out = mlp_all[:, :D]
    fc2_out = mlp_all[:, D:].transpose(0, 2, 1)
    return (
        output, tokens_grad, qkv_out, qv_out, table_out, proj_out, fc1_out, fc1_bias_out,
        fc2_out, gains_out, shifts_out,
    )


def solution(mesh):
    rows = P(("dp", "head"), None)
    placed = (
        rows,
        rows,
        P("dp", None),
        P(None, None, None, "head"),
        P(None, None, "head"),
        P(None, None, "head"),
        P(None, "head", None),
        P(None, None, "head"),
        P(None, "head"),
        P(None, "head", None),
        P(),
        P(),
    )
    return jax.shard_map(
        body,
        mesh=mesh,
        in_specs=placed,
        out_specs=(
            rows,
            rows,
            P(None, None, None, "head"),
            P(None, None, "head"),
            P(None, None, "head"),
            P(None, "head", None),
            P(None, None, "head"),
            P(None, "head"),
            P(None, "head", None),
            P(),
            P(),
        ),
        check_vma=False,
    )
```

time: 970 us -> 422 us (0.44)
  waiting for transfers between devices: 432 us -> 97.3 us
  Pallas kernels: 0 us -> 199 us
  local copies, waits for them, and re-layouts: 204 us -> 28.6 us
  matrix products: 148 us -> 4.56 us
  blocking collectives: 76.6 us -> 0 us
  other arithmetic: 85.8 us -> 14.8 us
  starting transfers between devices: 1.33 us -> 66.7 us
  between operations: 16.2 us -> 3.96 us
    reduce_scatter x8 -> x0, waiting for transfers between devices: 230 us -> none  [the longest x4 134 us: branch_total(): lax.psum_scatter(product(jnp.int32(0), lax.axis_size('head') * own_rows)....]
    pallas_call x0 -> x13, Pallas kernels: none -> 199 us  [the longest x2 65.1 us: attn_backward(): pl.pallas_call(kernel, out_shape=(jax.ShapeDtypeStruct((rows, D), F32), j...]
    all_gather x8 -> x0, waiting for transfers between devices: 170 us -> none  [the longest x4 87.5 us: norm_rows(): return lax.all_gather(values, 'head', axis=0, tiled=True)]
    dot_general x36 -> x3, matrix products: 139 us -> 4.56 us  [the longest x2 3 us: body(): jnp.einsum('nt,hn->ht', hot, dscores, precision=highest).reshape(4, 3, 169)]
    ppermute x0 -> x59, waiting for transfers between devices: none -> 97.3 us  [the longest x27 68.1 us: swap_dp(): return lax.ppermute(value, 'dp', [(i, i ^ step) for i in range(size)])]
    psum x2 -> x0, blocking collectives: 76.6 us -> none  [the longest x1 38.7 us: body(): lax.psum((qkv_total, qv_total, table_total, proj_total, fc1_total, fc1_bi...]
    ppermute x0 -> x59, starting transfers between devices: none -> 66.7 us  [the longest x27 44.8 us: swap_dp(): return lax.ppermute(value, 'dp', [(i, i ^ step) for i in range(size)])]
    reduce_sum x23 -> x0, other arithmetic: 40 us -> none  [the longest x2 6.14 us: body(): qv_grad = jnp.sum(stacked[:, 0::2].astype(wide_type), axis=0)]
  transfers between devices with their start and end apart: 17 -> 59, of which waited for: 16 -> 28; matrix products, arithmetic and copies ran while one was open for 11% -> 8% of each run, Pallas kernels for 0% -> 22%
where the time goes in v1:
time: 422 us; the launch traced here: 415 us
  Pallas kernels  199 us (47%)
  waiting for transfers between devices  97.3 us (23%)
  starting transfers between devices  66.7 us (16%)
  local copies, waits for them, and re-layouts  28.6 us (7%)
  other arithmetic  14.8 us (4%)
  matrix products  4.56 us (1%)
    ppermute x27, waiting for transfers between devices, swap_dp(): return lax.ppermute(value, 'dp', [(i, i ^ step) for i in range(size)])  68.1 us
    pallas_call x2, Pallas kernels, attn_backward(): pl.pallas_call(kernel, out_shape=(jax.ShapeDtypeStruct((rows, D), F32), j...  65.1 us
    pallas_call x2, Pallas kernels, attn_forward(): pl.pallas_call(kernel, out_shape=(jax.ShapeDtypeStruct((rows, D), F32), j...  62.2 us
    ppermute x27, starting transfers between devices, swap_dp(): return lax.ppermute(value, 'dp', [(i, i ^ step) for i in range(size)])  44.8 us
    ppermute x10, waiting for transfers between devices, swap_chip(): return lax.ppermute(value, 'head', [(i, i ^ 2) for i in range(4)])  28 us
    pallas_call x2, Pallas kernels, mlp_backward(): pl.pallas_call(kernel, out_shape=(jax.ShapeDtypeStruct((rows, D), F32), j...  27.9 us
    pallas_call x2, Pallas kernels, mlp_forward(): pl.pallas_call(kernel, out_shape=(jax.ShapeDtypeStruct((rows, D), F32), j...  26.4 us
    ppermute x10, starting transfers between devices, swap_chip(): return lax.ppermute(value, 'head', [(i, i ^ 2) for i in range(4)])  11.1 us
  transfers between devices with their start and end apart: 59, of which 28 were waited for; matrix products, arithmetic and copies ran while one was open for 8% of the time, Pallas kernels for 22%

profile of v1, /device:TPU:0, one launch (start us, length us, event | category | flops | bytes accessed | tf_op | source)
XLA Modules:
  0.0 415.1 jit_solution(1846380029599587450)
XLA Ops:
  3.3 2.7 collective-permute-start.2
  8.7 2.0 collective-permute-start.7
  16.9 3.8 plan.1.table_ref
  24.0 1.6 convolution_bitcast_fusion
  28.1 1.7 collective-permute-start.3
  30.5 2.6 collective-permute-start.4
  36.0 3.4 gather_slots.3
  40.3 3.5 gather_slots.2
  43.8 1.5 collective-permute-start.13
  45.4 28.8 %attn_forward.2 = (f32[1008,384]{1,0:T(8,128)}, bf16[1008,384]{1,0:T(8,128)(2,1)}, bf16[18,64,1152]{2,1,0:T(8,128)(2,1)}, bf16[18,3,64,256]{3,2,1,0:T(8,128)(2,1)}, bf16[1008,384]{1,0:T(8,128)(2,1)}) custom-call(s32[144]{0:T(256)} %plan.1.table_ref, f32[1008,384]{1,0:T(8,128)} %bitcast.159, bf16[384,384]{1,0:T(8,128)(2,1)} %copy-done.17, ...), custom_call_target="tpu_custom_call" | custom-call | flops 8000000000 | bytes 12000000 | tf_op jit(solution)/shard_map/attn_forward/pallas_call | solution.py:419
  76.1 13.2 %mlp_forward.2 = (f32[1008,384]{1,0:T(8,128)}, bf16[1008,384]{1,0:T(8,128)(2,1)}, bf16[1008,1536]{1,0:T(8,128)(2,1)}, bf16[1008,1536]{1,0:T(8,128)(2,1)}) custom-call(f32[1008,384]{1,0:T(8,128)} %get-tuple-element.49.mid_ref, bf16[768,384]{1,0:T(8,128)(2,1)} %pad_maximum_fusion.w0, bf16[768,384]{1,0:T(8,128)(2,1)} %collective-permute-done.7.w1, ...), custom_call_target="tpu_custom_call" | custom-call | flops 8000000000 | bytes 12000000 | tf_op jit(solution)/shard_map/mlp_forward/pallas_call | solution.py:605
  90.2 33.3 %attn_forward.3 = (f32[1008,384]{1,0:T(8,128)}, bf16[1008,384]{1,0:T(8,128)(2,1)}, bf16[18,64,1152]{2,1,0:T(8,128)(2,1)}, bf16[18,3,64,256]{3,2,1,0:T(8,128)(2,1)}, bf16[1008,384]{1,0:T(8,128)(2,1)}) custom-call(s32[144]{0:T(256)} %plan.1.table_ref, f32[1008,384]{1,0:T(8,128)} %get-tuple-element.50.hidden_ref, bf16[384,384]{1,0:T(8,128)(2,1)} %pad_maximum_fusion.3.w0, ...), custom_call_target="tpu_custom_call" | custom-call | flops 8000000000 | bytes 12000000 | tf_op jit(solution)/shard_map/attn_forward/pallas_call | solution.py:419
  124.6 13.2 %mlp_forward.3 = (f32[1008,384]{1,0:T(8,128)}, bf16[1008,384]{1,0:T(8,128)(2,1)}, bf16[1008,1536]{1,0:T(8,128)(2,1)}, bf16[1008,1536]{1,0:T(8,128)(2,1)}) custom-call(f32[1008,384]{1,0:T(8,128)} %get-tuple-element.51.mid_ref, bf16[768,384]{1,0:T(8,128)(2,1)} %pad_maximum_fusion.1.w0, bf16[768,384]{1,0:T(8,128)(2,1)} %copy-done.34, ...), custom_call_target="tpu_custom_call" | custom-call | flops 8000000000 | bytes 12000000 | tf_op jit(solution)/shard_map/mlp_forward/pallas_call | solution.py:605
  137.8 14.1 %mlp_backward.2 = (f32[1008,384]{1,0:T(8,128)}, bf16[2,768,384]{2,1,0:T(8,128)(2,1)}, bf16[2,768,384]{2,1,0:T(8,128)(2,1)}, f32[8,384]{1,0:T(8,128)}, f32[1,1536]{1,0:T(1,128)}) custom-call(f32[1008,384]{1,0:T(8,128)} %bitcast.158, f32[1008,384]{1,0:T(8,128)} %get-tuple-element.51.mid_ref, bf16[1008,384]{1,0:T(8,128)(2,1)} %get-tuple-element.53.a_ref, ...), custom_call_target="tpu_custom_call" | custom-call | flops 16000000000 | bytes 15000000 | tf_op jit(solution)/shard_map/mlp_backward/pallas_call | solution.py:663
  151.9 34.8 %attn_backward.2 = (f32[1008,384]{1,0:T(8,128)}, bf16[2,384,384]{2,1,0:T(8,128)(2,1)}, bf16[2,384,384]{2,1,0:T(8,128)(2,1)}, f32[8,384]{1,0:T(8,128)}, f32[3,56,256]{2,1,0:T(8,128)}) custom-call(s32[144]{0:T(256)} %plan.1.table_ref, f32[1008,384]{1,0:T(8,128)} %get-tuple-element.56.grad_ref, f32[1008,384]{1,0:T(8,128)} %get-tuple-element.50.hidden_ref, ...), custom_call_target="tpu_custom_call" | custom-call | flops 16000000000 | bytes 12000000 | tf_op jit(solution)/shard_map/attn_backward/pallas_call | solution.py:552
  188.2 13.7 %mlp_backward.3 = (f32[1008,384]{1,0:T(8,128)}, bf16[2,768,384]{2,1,0:T(8,128)(2,1)}, bf16[2,768,384]{2,1,0:T(8,128)(2,1)}, f32[8,384]{1,0:T(8,128)}, f32[1,1536]{1,0:T(1,128)}) custom-call(f32[1008,384]{1,0:T(8,128)} %get-tuple-element.61.grad_ref, f32[1008,384]{1,0:T(8,128)} %get-tuple-element.49.mid_ref, bf16[1008,384]{1,0:T(8,128)(2,1)} %get-tuple-element.62.a_ref, ...), custom_call_target="tpu_custom_call" | custom-call | flops 16000000000 | bytes 15000000 | tf_op jit(solution)/shard_map/mlp_backward/pallas_call | solution.py:663
  201.9 30.3 %attn_backward.3 = (f32[1008,384]{1,0:T(8,128)}, bf16[2,384,384]{2,1,0:T(8,128)(2,1)}, bf16[2,384,384]{2,1,0:T(8,128)(2,1)}, f32[8,384]{1,0:T(8,128)}, f32[3,56,256]{2,1,0:T(8,128)}) custom-call(s32[144]{0:T(256)} %plan.1.table_ref, f32[1008,384]{1,0:T(8,128)} %get-tuple-element.65.grad_ref, f32[1008,384]{1,0:T(8,128)} %bitcast.160, ...), custom_call_target="tpu_custom_call" | custom-call | flops 16000000000 | bytes 12000000 | tf_op jit(solution)/shard_map/attn_backward/pallas_call | solution.py:552
  234.2 1.5 fusion.17
  236.6 1.5 fusion.16
  241.4 3.4 collective-permute-done.39
  244.8 1.5 collective-permute-start.40
  249.0 1.8 collective-permute-start.41
  253.0 2.8 collective-permute-start.42
  261.6 1.4 convert_add_fusion.2
  265.1 6.9 %collective-permute-done.31 = bf16[384,384]{1,0:T(8,128)(2,1)S(1)} collective-permute-done((bf16[384,384]{1,0:T(8,128)(2,1)S(1)}, bf16[384,384]{1,0:T(8,128)(2,1)S(1)}, u32[]{:S(2)}, u32[]{:S(2)}) %collective-permute-start.31) | collective-permute-done | bytes 294944 | tf_op jit(solution)/shard_map/ppermute | solution.py:691
  272.9 7.2 %collective-permute-done.23 = bf16[384,384]{1,0:T(8,128)(2,1)S(1)} collective-permute-done((bf16[384,384]{1,0:T(8,128)(2,1)S(1)}, bf16[384,384]{1,0:T(8,128)(2,1)S(1)}, u32[]{:S(2)}, u32[]{:S(2)}) %collective-permute-start.23) | collective-permute-done | bytes 294944 | tf_op jit(solution)/shard_map/ppermute | solution.py:691
  281.4 4.1 collective-permute-done.32
  286.8 3.8 collective-permute-done.24
  290.7 1.7 collective-permute-start.33
  292.5 2.6 collective-permute-done.33
  295.0 1.7 collective-permute-start.25
  296.8 2.6 collective-permute-done.25
  299.4 2.8 collective-permute-start.34
  302.3 2.0 collective-permute-done.34
  304.3 2.9 collective-permute-start.26
  307.1 2.0 collective-permute-done.26
  309.1 2.9 collective-permute-start.35
  312.0 2.1 collective-permute-done.35
  314.1 2.8 collective-permute-start.27
  316.9 2.1 collective-permute-done.27
  318.9 2.0 collective-permute-start.36
  321.1 1.5 convert_add_fusion
  326.5 2.8 collective-permute-done.37
  330.1 3.6 collective-permute-done.52
  335.1 6.9 %collective-permute-done.44 = bf16[768,384]{1,0:T(8,128)(2,1)S(1)} collective-permute-done((bf16[768,384]{1,0:T(8,128)(2,1)S(1)}, bf16[768,384]{1,0:T(8,128)(2,1)S(1)}, u32[]{:S(2)}, u32[]{:S(2)}) %collective-permute-start.44) | collective-permute-done | bytes 589856 | tf_op jit(solution)/shard_map/ppermute | solution.py:691
  343.4 6.7 %collective-permute-done.53 = bf16[384,384]{1,0:T(8,128)(2,1)S(1)} collective-permute-done((bf16[384,384]{1,0:T(8,128)(2,1)S(1)}, bf16[384,384]{1,0:T(8,128)(2,1)S(1)}, u32[]{:S(2)}, u32[]{:S(2)}) %collective-permute-start.53) | collective-permute-done | bytes 294944 | tf_op jit(solution)/shard_map/ppermute | solution.py:699
  351.4 5.4 %collective-permute-done.45 = bf16[384,384]{1,0:T(8,128)(2,1)S(1)} collective-permute-done((bf16[384,384]{1,0:T(8,128)(2,1)S(1)}, bf16[384,384]{1,0:T(8,128)(2,1)S(1)}, u32[]{:S(2)}, u32[]{:S(2)}) %collective-permute-start.45) | collective-permute-done | bytes 294944 | tf_op jit(solution)/shard_map/ppermute | solution.py:699
  356.8 2.0 collective-permute-start.54
  358.9 3.9 collective-permute-done.54
  362.8 1.4 collective-permute-start.46
  364.2 3.7 collective-permute-done.46
  367.9 2.5 collective-permute-start.55
  370.4 4.7 %collective-permute-done.55 = bf16[96,384]{1,0:T(8,128)(2,1)S(1)} collective-permute-done((bf16[96,384]{1,0:T(8,128)(2,1)S(1)}, bf16[96,384]{1,0:T(8,128)(2,1)S(1)}, u32[]{:S(2)}, u32[]{:S(2)}) %collective-permute-start.55) | collective-permute-done | bytes 73760 | tf_op jit(solution)/shard_map/ppermute | solution.py:699
  376.2 4.3 %collective-permute-done.47 = bf16[96,384]{1,0:T(8,128)(2,1)S(1)} collective-permute-done((bf16[96,384]{1,0:T(8,128)(2,1)S(1)}, bf16[96,384]{1,0:T(8,128)(2,1)S(1)}, u32[]{:S(2)}, u32[]{:S(2)}) %collective-permute-start.47) | collective-permute-done | bytes 73760 | tf_op jit(solution)/shard_map/ppermute | solution.py:699
  380.5 1.7 collective-permute-start.56
  382.2 3.5 collective-permute-done.56
  385.7 1.7 collective-permute-start.48
  387.5 3.5 collective-permute-done.48
  391.0 2.0 collective-permute-start.57
  393.2 2.9 collective-permute-done.57
  402.2 3.4 return_slots.2
  406.3 3.4 return_slots.3
  409.9 2.0 collective-permute-done.50
  413.5 1.4 copy.47
  (315 shorter events, 65.9 us)
Async XLA Ops:
  0.7 38.8 %collective-permute-start = (f32[784,384]{1,0:T(8,128)}, f32[784,384]{1,0:T(8,128)}, u32[]{:S(2)}, u32[]{:S(2)}) collective-permute-start(f32[784,384]{1,0:T(8,128)} %mine_ref.2), channel_id=1, source_target_pairs={{0,1},{1,0},{2,3},{3,2},{4,5},{5,4},{6,7},{7,6},{8,9},{9,8},{10,11... | collective-permute-start | bytes 3612680 | tf_op jit(solution)/shard_map/ppermute | solution.py:687
  3.3 24.8 %copy-start.17 = (bf16[384,384]{1,0:T(8,128)(2,1)}, bf16[384,384]{1,0:T(8,128)(2,1)S(1)}, u32[]{:S(2)}) copy-start(bf16[384,384]{1,0:T(8,128)(2,1)S(1)} %pad_maximum_fusion.2.w0) | copy-start | bytes 884740
  3.3 26.5 %collective-permute-start.2 = (bf16[384,384]{1,0:T(8,128)(2,1)S(1)}, bf16[384,384]{1,0:T(8,128)(2,1)}, u32[]{:S(2)}, u32[]{:S(2)}) collective-permute-start(bf16[384,384]{1,0:T(8,128)(2,1)S(1)} %pad_maximum_fusion.2.w0), channel_id=1, source_target_pairs={{0,2},{1,3},{2,0},{3,1},{4,6},{5,7},{6,4},{7,5},{8,10},{9,11},{10,... | collective-permute-start | bytes 884744 | tf_op jit(solution)/shard_map/ppermute | solution.py:691
  6.4 9.2 %collective-permute-start.5 = (f32[6,384]{1,0:T(8,128)S(1)}, f32[6,384]{1,0:T(8,128)S(1)}, u32[]{:S(2)}, u32[]{:S(2)}) collective-permute-start(f32[6,384]{1,0:T(8,128)S(1)} %get-tuple-element.145), channel_id=1, source_target_pairs={{0,2},{1,3},{2,0},{3,1},{4,6},{5,7},{6,4},{7,5},{8,10},{9,11},{10,... | collective-permute-start | bytes 27656 | tf_op jit(solution)/shard_map/ppermute | solution.py:691
  8.7 36.6 %collective-permute-start.7 = (bf16[768,384]{1,0:T(8,128)(2,1)}, bf16[768,384]{1,0:T(8,128)(2,1)}, u32[]{:S(2)}, u32[]{:S(2)}) collective-permute-start(bf16[768,384]{1,0:T(8,128)(2,1)} %pad_maximum_fusion.w0), channel_id=1, source_target_pairs={{0,2},{1,3},{2,0},{3,1},{4,6},{5,7},{6,4},{7,5},{8,10},{9,11},{10,... | collective-permute-start | bytes 1769480 | tf_op jit(solution)/shard_map/ppermute | solution.py:691
  10.7 19.8 %collective-permute-start.18 = (bf16[784,384]{1,0:T(8,128)(2,1)S(1)}, bf16[784,384]{1,0:T(8,128)(2,1)}, u32[]{:S(2)}, u32[]{:S(2)}) collective-permute-start(bf16[784,384]{1,0:T(8,128)(2,1)S(1)} %copy-done.5), channel_id=1, source_target_pairs={{0,1},{1,0},{2,3},{3,2},{4,5},{5,4},{6,7},{7,6},{8,9},{9,8},{10,11... | collective-permute-start | bytes 1806344 | tf_op jit(solution)/shard_map/ppermute | solution.py:687
  15.7 5.1 %collective-permute-start.6 = (f32[2,6,384]{2,0,1:T(2,128)S(1)}, f32[2,6,384]{2,0,1:T(2,128)S(1)}, u32[]{:S(2)}, u32[]{:S(2)}) collective-permute-start(f32[2,6,384]{2,0,1:T(2,128)S(1)} %pad_maximum_fusion.8), channel_id=1, source_target_pairs={{0,1},{1,0},{2,3},{3,2},{4,5},{5,4},{6,7},{7,6},{8,9},{9,8},{10,11... | collective-permute-start | bytes 55304 | tf_op jit(solution)/shard_map/ppermute | solution.py:687
  20.8 7.2 %collective-permute-start.19 = (bf16[196,384]{1,0:T(8,128)(2,1)}, bf16[196,384]{1,0:T(8,128)(2,1)S(1)}, u32[]{:S(2)}, u32[]{:S(2)}) collective-permute-start(bf16[196,384]{1,0:T(8,128)(2,1)} %slice_select_fusion.1), channel_id=1, source_target_pairs={{1,2},{2,1},{5,6},{6,5},{9,10},{10,9},{13,14},{14,13},{17,18},{18,... | collective-permute-start | bytes 451592 | tf_op jit(solution)/shard_map/ppermute | solution.py:695
  28.1 15.7 %collective-permute-start.3 = (bf16[384,384]{1,0:T(8,128)(2,1)S(1)}, bf16[384,384]{1,0:T(8,128)(2,1)}, u32[]{:S(2)}, u32[]{:S(2)}) collective-permute-start(bf16[384,384]{1,0:T(8,128)(2,1)S(1)} %pad_maximum_fusion.2.w0), channel_id=1, source_target_pairs={{0,1},{1,0},{2,3},{3,2},{4,5},{5,4},{6,7},{7,6},{8,9},{9,8},{10,11... | collective-permute-start | bytes 884744 | tf_op jit(solution)/shard_map/ppermute | solution.py:687
  29.8 9.6 %collective-permute-start.1 = (f32[196,384]{1,0:T(8,128)S(1)}, f32[196,384]{1,0:T(8,128)S(1)}, u32[]{:S(2)}, u32[]{:S(2)}) collective-permute-start(f32[196,384]{1,0:T(8,128)S(1)} %copy-done.15), channel_id=1, source_target_pairs={{1,2},{2,1},{5,6},{6,5},{9,10},{10,9},{13,14},{14,13},{17,18},{18,... | collective-permute-start | bytes 903176 | tf_op jit(solution)/shard_map/ppermute | solution.py:695
  30.5 13.3 %collective-permute-start.4 = (bf16[384,384]{1,0:T(8,128)(2,1)}, bf16[384,384]{1,0:T(8,128)(2,1)S(1)}, u32[]{:S(2)}, u32[]{:S(2)}) collective-permute-start(bf16[384,384]{1,0:T(8,128)(2,1)} %collective-permute-done.2.w1), channel_id=1, source_target_pairs={{0,1},{1,0},{2,3},{3,2},{4,5},{5,4},{6,7},{7,6},{8,9},{9,8},{10,11... | collective-permute-start | bytes 884744 | tf_op jit(solution)/shard_map/ppermute | solution.py:687
  39.4 35.4 %collective-permute-start.8 = (bf16[768,384]{1,0:T(8,128)(2,1)}, bf16[768,384]{1,0:T(8,128)(2,1)S(1)}, u32[]{:S(2)}, u32[]{:S(2)}) collective-permute-start(bf16[768,384]{1,0:T(8,128)(2,1)} %pad_maximum_fusion.w0), channel_id=1, source_target_pairs={{0,1},{1,0},{2,3},{3,2},{4,5},{5,4},{6,7},{7,6},{8,9},{9,8},{10,11... | collective-permute-start | bytes 1769480 | tf_op jit(solution)/shard_map/ppermute | solution.py:687
  39.5 34.7 %collective-permute-start.10 = (bf16[384,384]{1,0:T(8,128)(2,1)S(1)}, bf16[384,384]{1,0:T(8,128)(2,1)S(1)}, u32[]{:S(2)}, u32[]{:S(2)}) collective-permute-start(bf16[384,384]{1,0:T(8,128)(2,1)S(1)} %copy-done.18), channel_id=1, source_target_pairs={{0,2},{1,3},{2,0},{3,1},{4,6},{5,7},{6,4},{7,5},{8,10},{9,11},{10,... | collective-permute-start | bytes 884744 | tf_op jit(solution)/shard_map/ppermute | solution.py:691
  43.8 45.5 %collective-permute-start.11 = (bf16[384,384]{1,0:T(8,128)(2,1)S(1)}, bf16[384,384]{1,0:T(8,128)(2,1)S(1)}, u32[]{:S(2)}, u32[]{:S(2)}) collective-permute-start(bf16[384,384]{1,0:T(8,128)(2,1)S(1)} %copy-done.18), channel_id=1, source_target_pairs={{0,1},{1,0},{2,3},{3,2},{4,5},{5,4},{6,7},{7,6},{8,9},{9,8},{10,11... | collective-permute-start | bytes 884744 | tf_op jit(solution)/shard_map/ppermute | solution.py:687
  43.8 31.0 %collective-permute-start.13 = (bf16[768,384]{1,0:T(8,128)(2,1)S(1)}, bf16[768,384]{1,0:T(8,128)(2,1)S(1)}, u32[]{:S(2)}, u32[]{:S(2)}) collective-permute-start(bf16[768,384]{1,0:T(8,128)(2,1)S(1)} %copy-done.8), channel_id=1, source_target_pairs={{0,2},{1,3},{2,0},{3,1},{4,6},{5,7},{6,4},{7,5},{8,10},{9,11},{10,... | collective-permute-start | bytes 1769480 | tf_op jit(solution)/shard_map/ppermute | solution.py:691
  45.3 30.0 %collective-permute-start.9 = (bf16[768,384]{1,0:T(8,128)(2,1)}, bf16[768,384]{1,0:T(8,128)(2,1)S(1)}, u32[]{:S(2)}, u32[]{:S(2)}) collective-permute-start(bf16[768,384]{1,0:T(8,128)(2,1)} %collective-permute-done.7.w1), channel_id=1, source_target_pairs={{0,1},{1,0},{2,3},{3,2},{4,5},{5,4},{6,7},{7,6},{8,9},{9,8},{10,11... | collective-permute-start | bytes 1769480 | tf_op jit(solution)/shard_map/ppermute | solution.py:687
  74.2 15.1 %copy-start.38 = (bf16[384,384]{1,0:T(8,128)(2,1)}, bf16[384,384]{1,0:T(8,128)(2,1)S(1)}, u32[]{:S(2)}) copy-start(bf16[384,384]{1,0:T(8,128)(2,1)S(1)} %collective-permute-done.10.w1) | copy-start | bytes 884740
  74.3 49.3 %collective-permute-start.14 = (bf16[768,384]{1,0:T(8,128)(2,1)S(1)}, bf16[768,384]{1,0:T(8,128)(2,1)S(1)}, u32[]{:S(2)}, u32[]{:S(2)}) collective-permute-start(bf16[768,384]{1,0:T(8,128)(2,1)S(1)} %copy-done.8), channel_id=1, source_target_pairs={{0,1},{1,0},{2,3},{3,2},{4,5},{5,4},{6,7},{7,6},{8,9},{9,8},{10,11... | collective-permute-start | bytes 1769480 | tf_op jit(solution)/shard_map/ppermute | solution.py:687
  74.8 14.6 %collective-permute-start.12 = (bf16[384,384]{1,0:T(8,128)(2,1)S(1)}, bf16[384,384]{1,0:T(8,128)(2,1)S(1)}, u32[]{:S(2)}, u32[]{:S(2)}) collective-permute-start(bf16[384,384]{1,0:T(8,128)(2,1)S(1)} %collective-permute-done.10.w1), channel_id=1, source_target_pairs={{0,1},{1,0},{2,3},{3,2},{4,5},{5,4},{6,7},{7,6},{8,9},{9,8},{10,11... | collective-permute-start | bytes 884744 | tf_op jit(solution)/shard_map/ppermute | solution.py:687
  74.9 48.7 %collective-permute-start.15 = (bf16[768,384]{1,0:T(8,128)(2,1)S(1)}, bf16[768,384]{1,0:T(8,128)(2,1)S(1)}, u32[]{:S(2)}, u32[]{:S(2)}) collective-permute-start(bf16[768,384]{1,0:T(8,128)(2,1)S(1)} %collective-permute-done.13.w1), channel_id=1, source_target_pairs={{0,1},{1,0},{2,3},{3,2},{4,5},{5,4},{6,7},{7,6},{8,9},{9,8},{10,11... | collective-permute-start | bytes 1769480 | tf_op jit(solution)/shard_map/ppermute | solution.py:687
  201.9 31.8 %copy-start.20 = (f32[3,56,256]{2,1,0:T(8,128)S(1)}, f32[3,56,256]{2,1,0:T(8,128)}, u32[]{:S(2)}) copy-start(f32[3,56,256]{2,1,0:T(8,128)} %get-tuple-element.82) | copy-start | bytes 516100
  239.4 1.3 collective-permute-start.38
  240.7 4.0 collective-permute-start.39
  244.8 4.2 %collective-permute-start.40 = (f32[20,384]{1,0:T(8,128)S(1)}, f32[20,384]{1,0:T(8,128)S(1)}, u32[]{:S(2)}, u32[]{:S(2)}) collective-permute-start(f32[20,384]{1,0:T(8,128)S(1)} %fusion.8), channel_id=1, source_target_pairs={{0,4},{4,0},{8,12},{12,8},{16,20},{20,16},{24,28},{28,24},{1,5},{5... | collective-permute-start | bytes 92168 | tf_op jit(solution)/shard_map/ppermute | solution.py:699
  248.9 153.3 %collective-permute-start.16 = (f32[18,56,384]{2,1,0:T(8,128)S(1)}, f32[18,56,384]{2,1,0:T(8,128)}, u32[]{:S(2)}, u32[]{:S(2)}) collective-permute-start(f32[18,56,384]{2,1,0:T(8,128)S(1)} %bitcast.153), channel_id=1, source_target_pairs={{0,1},{1,0},{2,3},{3,2},{4,5},{5,4},{6,7},{7,6},{8,9},{9,8},{10,11... | collective-permute-start | bytes 4644872 | tf_op jit(solution)/shard_map/ppermute | solution.py:687
  249.0 4.0 collective-permute-start.41
  251.5 154.1 %collective-permute-start.20 = (f32[18,56,384]{2,1,0:T(8,128)S(1)}, f32[18,56,384]{2,1,0:T(8,128)}, u32[]{:S(2)}, u32[]{:S(2)}) collective-permute-start(f32[18,56,384]{2,1,0:T(8,128)S(1)} %bitcast.156), channel_id=1, source_target_pairs={{0,1},{1,0},{2,3},{3,2},{4,5},{5,4},{6,7},{7,6},{8,9},{9,8},{10,11... | collective-permute-start | bytes 4644872 | tf_op jit(solution)/shard_map/ppermute | solution.py:687
  253.0 4.9 %collective-permute-start.42 = (f32[20,384]{1,0:T(8,128)S(1)}, f32[20,384]{1,0:T(8,128)S(1)}, u32[]{:S(2)}, u32[]{:S(2)}) collective-permute-start(f32[20,384]{1,0:T(8,128)S(1)} %add.206), channel_id=1, source_target_pairs={{0,16},{4,20},{8,24},{12,28},{16,0},{20,4},{24,8},{28,12},{1,17},{... | collective-permute-start | bytes 92168 | tf_op jit(solution)/shard_map/ppermute | solution.py:699
  256.5 4.5 %collective-permute-start.30 = (bf16[2,384,384]{2,1,0:T(8,128)(2,1)}, bf16[2,384,384]{2,1,0:T(8,128)(2,1)}, u32[]{:S(2)}, u32[]{:S(2)}) collective-permute-start(bf16[2,384,384]{2,1,0:T(8,128)(2,1)} %get-tuple-element.74), channel_id=1, source_target_pairs={{0,1},{1,0},{2,3},{3,2},{4,5},{5,4},{6,7},{7,6},{8,9},{9,8},{10,11... | collective-permute-start | bytes 1769480 | tf_op jit(solution)/shard_map/ppermute | solution.py:687
  256.5 6.5 %collective-permute-start.22 = (bf16[2,384,384]{2,1,0:T(8,128)(2,1)}, bf16[2,384,384]{2,1,0:T(8,128)(2,1)}, u32[]{:S(2)}, u32[]{:S(2)}) collective-permute-start(bf16[2,384,384]{2,1,0:T(8,128)(2,1)} %get-tuple-element.72), channel_id=1, source_target_pairs={{0,1},{1,0},{2,3},{3,2},{4,5},{5,4},{6,7},{7,6},{8,9},{9,8},{10,11... | collective-permute-start | bytes 1769480 | tf_op jit(solution)/shard_map/ppermute | solution.py:687
  257.8 63.1 %collective-permute-start.51 = (bf16[2,768,384]{2,1,0:T(8,128)(2,1)}, bf16[2,768,384]{2,1,0:T(8,128)(2,1)}, u32[]{:S(2)}, u32[]{:S(2)}) collective-permute-start(bf16[2,768,384]{2,1,0:T(8,128)(2,1)} %get-tuple-element.86), channel_id=1, source_target_pairs={{0,1},{1,0},{2,3},{3,2},{4,5},{5,4},{6,7},{7,6},{8,9},{9,8},{10,11... | collective-permute-start | bytes 3538952 | tf_op jit(solution)/shard_map/ppermute | solution.py:687
  261.1 61.6 %collective-permute-start.43 = (bf16[2,768,384]{2,1,0:T(8,128)(2,1)}, bf16[2,768,384]{2,1,0:T(8,128)(2,1)S(1)}, u32[]{:S(2)}, u32[]{:S(2)}) collective-permute-start(bf16[2,768,384]{2,1,0:T(8,128)(2,1)} %get-tuple-element.84), channel_id=1, source_target_pairs={{0,1},{1,0},{2,3},{3,2},{4,5},{5,4},{6,7},{7,6},{8,9},{9,8},{10,11... | collective-permute-start | bytes 3538952 | tf_op jit(solution)/shard_map/ppermute | solution.py:687
  263.1 9.0 %collective-permute-start.31 = (bf16[384,384]{1,0:T(8,128)(2,1)S(1)}, bf16[384,384]{1,0:T(8,128)(2,1)S(1)}, u32[]{:S(2)}, u32[]{:S(2)}) collective-permute-start(bf16[384,384]{1,0:T(8,128)(2,1)S(1)} %fusion.7), channel_id=1, source_target_pairs={{0,2},{1,3},{2,0},{3,1},{4,6},{5,7},{6,4},{7,5},{8,10},{9,11},{10,... | collective-permute-start | bytes 884744 | tf_op jit(solution)/shard_map/ppermute | solution.py:691
  272.0 8.1 %collective-permute-start.23 = (bf16[384,384]{1,0:T(8,128)(2,1)S(1)}, bf16[384,384]{1,0:T(8,128)(2,1)S(1)}, u32[]{:S(2)}, u32[]{:S(2)}) collective-permute-start(bf16[384,384]{1,0:T(8,128)(2,1)S(1)} %fusion.6), channel_id=1, source_target_pairs={{0,2},{1,3},{2,0},{3,1},{4,6},{5,7},{6,4},{7,5},{8,10},{9,11},{10,... | collective-permute-start | bytes 884744 | tf_op jit(solution)/shard_map/ppermute | solution.py:691
  280.1 5.4 %collective-permute-start.32 = (bf16[192,384]{1,0:T(8,128)(2,1)S(1)}, bf16[192,384]{1,0:T(8,128)(2,1)S(1)}, u32[]{:S(2)}, u32[]{:S(2)}) collective-permute-start(bf16[192,384]{1,0:T(8,128)(2,1)S(1)} %dynamic-slice_convert_fusion.4), channel_id=1, source_target_pairs={{0,4},{4,0},{8,12},{12,8},{16,20},{20,16},{24,28},{28,24},{1,5},{5... | collective-permute-start | bytes 442376 | tf_op jit(solution)/shard_map/ppermute | solution.py:699
  285.5 5.1 %collective-permute-start.24 = (bf16[192,384]{1,0:T(8,128)(2,1)S(1)}, bf16[192,384]{1,0:T(8,128)(2,1)S(1)}, u32[]{:S(2)}, u32[]{:S(2)}) collective-permute-start(bf16[192,384]{1,0:T(8,128)(2,1)S(1)} %dynamic-slice_convert_fusion.5), channel_id=1, source_target_pairs={{0,4},{4,0},{8,12},{12,8},{16,20},{20,16},{24,28},{28,24},{1,5},{5... | collective-permute-start | bytes 442376 | tf_op jit(solution)/shard_map/ppermute | solution.py:699
  286.8 34.2 %copy-start.6 = (bf16[2,768,384]{2,1,0:T(8,128)(2,1)S(1)}, bf16[2,768,384]{2,1,0:T(8,128)(2,1)}, u32[]{:S(2)}) copy-start(bf16[2,768,384]{2,1,0:T(8,128)(2,1)} %get-tuple-element.85) | copy-start | bytes 3538948
  290.7 4.4 %collective-permute-start.33 = (bf16[96,384]{1,0:T(8,128)(2,1)S(1)}, bf16[96,384]{1,0:T(8,128)(2,1)S(1)}, u32[]{:S(2)}, u32[]{:S(2)}) collective-permute-start(bf16[96,384]{1,0:T(8,128)(2,1)S(1)} %dynamic-slice_convert_fusion.8), channel_id=1, source_target_pairs={{0,8},{4,12},{8,0},{12,4},{16,24},{20,28},{24,16},{28,20},{1,9},{5... | collective-permute-start | bytes 221192 | tf_op jit(solution)/shard_map/ppermute | solution.py:699
  295.0 4.4 %collective-permute-start.25 = (bf16[96,384]{1,0:T(8,128)(2,1)S(1)}, bf16[96,384]{1,0:T(8,128)(2,1)S(1)}, u32[]{:S(2)}, u32[]{:S(2)}) collective-permute-start(bf16[96,384]{1,0:T(8,128)(2,1)S(1)} %dynamic-slice_convert_fusion.9), channel_id=1, source_target_pairs={{0,8},{4,12},{8,0},{12,4},{16,24},{20,28},{24,16},{28,20},{1,9},{5... | collective-permute-start | bytes 221192 | tf_op jit(solution)/shard_map/ppermute | solution.py:699
  299.4 4.9 %collective-permute-start.34 = (bf16[48,384]{1,0:T(8,128)(2,1)S(1)}, bf16[48,384]{1,0:T(8,128)(2,1)S(1)}, u32[]{:S(2)}, u32[]{:S(2)}) collective-permute-start(bf16[48,384]{1,0:T(8,128)(2,1)S(1)} %dynamic-slice_convert_fusion.10), channel_id=1, source_target_pairs={{0,16},{4,20},{8,24},{12,28},{16,0},{20,4},{24,8},{28,12},{1,17},{... | collective-permute-start | bytes 110600 | tf_op jit(solution)/shard_map/ppermute | solution.py:699
  304.3 4.9 %collective-permute-start.26 = (bf16[48,384]{1,0:T(8,128)(2,1)S(1)}, bf16[48,384]{1,0:T(8,128)(2,1)S(1)}, u32[]{:S(2)}, u32[]{:S(2)}) collective-permute-start(bf16[48,384]{1,0:T(8,128)(2,1)S(1)} %dynamic-slice_convert_fusion.11), channel_id=1, source_target_pairs={{0,16},{4,20},{8,24},{12,28},{16,0},{20,4},{24,8},{28,12},{1,17},{... | collective-permute-start | bytes 110600 | tf_op jit(solution)/shard_map/ppermute | solution.py:699
  309.1 5.0 %collective-permute-start.35 = (bf16[48,384]{1,0:T(8,128)(2,1)S(1)}, bf16[48,384]{1,0:T(8,128)(2,1)S(1)}, u32[]{:S(2)}, u32[]{:S(2)}) collective-permute-start(bf16[48,384]{1,0:T(8,128)(2,1)S(1)} %add_convert_fusion.2), channel_id=1, source_target_pairs={{0,16},{4,20},{8,24},{12,28},{16,0},{20,4},{24,8},{28,12},{1,17},{... | collective-permute-start | bytes 110600 | tf_op jit(solution)/shard_map/ppermute | solution.py:699
  314.1 4.9 %collective-permute-start.27 = (bf16[48,384]{1,0:T(8,128)(2,1)S(1)}, bf16[48,384]{1,0:T(8,128)(2,1)S(1)}, u32[]{:S(2)}, u32[]{:S(2)}) collective-permute-start(bf16[48,384]{1,0:T(8,128)(2,1)S(1)} %add_convert_fusion.3), channel_id=1, source_target_pairs={{0,16},{4,20},{8,24},{12,28},{16,0},{20,4},{24,8},{28,12},{1,17},{... | collective-permute-start | bytes 110600 | tf_op jit(solution)/shard_map/ppermute | solution.py:699
  318.9 5.2 %collective-permute-start.36 = (bf16[96,384]{1,0:T(8,128)(2,1)S(1)}, bf16[96,384]{1,0:T(8,128)(2,1)S(1)}, u32[]{:S(2)}, u32[]{:S(2)}) collective-permute-start(bf16[96,384]{1,0:T(8,128)(2,1)S(1)} %maximum_select_fusion.11), channel_id=1, source_target_pairs={{0,8},{4,12},{8,0},{12,4},{16,24},{20,28},{24,16},{28,20},{1,9},{5... | collective-permute-start | bytes 221192 | tf_op jit(solution)/shard_map/ppermute | solution.py:699
  320.9 4.5 %collective-permute-start.28 = (bf16[96,384]{1,0:T(8,128)(2,1)S(1)}, bf16[96,384]{1,0:T(8,128)(2,1)S(1)}, u32[]{:S(2)}, u32[]{:S(2)}) collective-permute-start(bf16[96,384]{1,0:T(8,128)(2,1)S(1)} %maximum_select_fusion.10), channel_id=1, source_target_pairs={{0,8},{4,12},{8,0},{12,4},{16,24},{20,28},{24,16},{28,20},{1,9},{5... | collective-permute-start | bytes 221192 | tf_op jit(solution)/shard_map/ppermute | solution.py:699
  322.7 11.0 %collective-permute-start.52 = (bf16[768,384]{1,0:T(8,128)(2,1)S(1)}, bf16[768,384]{1,0:T(8,128)(2,1)S(1)}, u32[]{:S(2)}, u32[]{:S(2)}) collective-permute-start(bf16[768,384]{1,0:T(8,128)(2,1)S(1)} %fusion.3), channel_id=1, source_target_pairs={{0,2},{1,3},{2,0},{3,1},{4,6},{5,7},{6,4},{7,5},{8,10},{9,11},{10,... | collective-permute-start | bytes 1769480 | tf_op jit(solution)/shard_map/ppermute | solution.py:691
  324.1 5.2 %collective-permute-start.37 = (bf16[192,384]{1,0:T(8,128)(2,1)S(1)}, bf16[192,384]{1,0:T(8,128)(2,1)S(1)}, u32[]{:S(2)}, u32[]{:S(2)}) collective-permute-start(bf16[192,384]{1,0:T(8,128)(2,1)S(1)} %maximum_select_fusion.7), channel_id=1, source_target_pairs={{0,4},{4,0},{8,12},{12,8},{16,20},{20,16},{24,28},{28,24},{1,5},{5... | collective-permute-start | bytes 442376 | tf_op jit(solution)/shard_map/ppermute | solution.py:699
  325.5 16.5 %collective-permute-start.44 = (bf16[768,384]{1,0:T(8,128)(2,1)S(1)}, bf16[768,384]{1,0:T(8,128)(2,1)S(1)}, u32[]{:S(2)}, u32[]{:S(2)}) collective-permute-start(bf16[768,384]{1,0:T(8,128)(2,1)S(1)} %fusion.2), channel_id=1, source_target_pairs={{0,2},{1,3},{2,0},{3,1},{4,6},{5,7},{6,4},{7,5},{8,10},{9,11},{10,... | collective-permute-start | bytes 1769480 | tf_op jit(solution)/shard_map/ppermute | solution.py:691
  329.3 70.2 %collective-permute-start.17 = (f32[4,56,384]{2,1,0:T(8,128)S(1)}, f32[4,56,384]{2,1,0:T(8,128)S(1)}, u32[]{:S(2)}, u32[]{:S(2)}) collective-permute-start(f32[4,56,384]{2,1,0:T(8,128)S(1)} %copy-done.12), channel_id=1, source_target_pairs={{1,2},{2,1},{5,6},{6,5},{9,10},{10,9},{13,14},{14,13},{17,18},{18,... | collective-permute-start | bytes 1032200 | tf_op jit(solution)/shard_map/ppermute | solution.py:695
  333.7 59.3 %collective-permute-start.29 = (bf16[192,384]{1,0:T(8,128)(2,1)S(1)}, bf16[192,384]{1,0:T(8,128)(2,1)S(1)}, u32[]{:S(2)}, u32[]{:S(2)}) collective-permute-start(bf16[192,384]{1,0:T(8,128)(2,1)S(1)} %maximum_select_fusion.6), channel_id=1, source_target_pairs={{0,4},{4,0},{8,12},{12,8},{16,20},{20,16},{24,28},{28,24},{1,5},{5... | collective-permute-start | bytes 442376 | tf_op jit(solution)/shard_map/ppermute | solution.py:699
  342.0 8.1 %collective-permute-start.53 = (bf16[384,384]{1,0:T(8,128)(2,1)S(1)}, bf16[384,384]{1,0:T(8,128)(2,1)S(1)}, u32[]{:S(2)}, u32[]{:S(2)}) collective-permute-start(bf16[384,384]{1,0:T(8,128)(2,1)S(1)} %dynamic-slice_convert_fusion), channel_id=1, source_target_pairs={{0,4},{4,0},{8,12},{12,8},{16,20},{20,16},{24,28},{28,24},{1,5},{5... | collective-permute-start | bytes 884744 | tf_op jit(solution)/shard_map/ppermute | solution.py:699
  350.1 6.7 %collective-permute-start.45 = (bf16[384,384]{1,0:T(8,128)(2,1)S(1)}, bf16[384,384]{1,0:T(8,128)(2,1)S(1)}, u32[]{:S(2)}, u32[]{:S(2)}) collective-permute-start(bf16[384,384]{1,0:T(8,128)(2,1)S(1)} %dynamic-slice_convert_fusion.1), channel_id=1, source_target_pairs={{0,4},{4,0},{8,12},{12,8},{16,20},{20,16},{24,28},{28,24},{1,5},{5... | collective-permute-start | bytes 884744 | tf_op jit(solution)/shard_map/ppermute | solution.py:699
  356.8 5.9 %collective-permute-start.54 = (bf16[192,384]{1,0:T(8,128)(2,1)S(1)}, bf16[192,384]{1,0:T(8,128)(2,1)S(1)}, u32[]{:S(2)}, u32[]{:S(2)}) collective-permute-start(bf16[192,384]{1,0:T(8,128)(2,1)S(1)} %dynamic-slice_convert_fusion.2), channel_id=1, source_target_pairs={{0,8},{4,12},{8,0},{12,4},{16,24},{20,28},{24,16},{28,20},{1,9},{5... | collective-permute-start | bytes 442376 | tf_op jit(solution)/shard_map/ppermute | solution.py:699
  362.8 5.1 %collective-permute-start.46 = (bf16[192,384]{1,0:T(8,128)(2,1)S(1)}, bf16[192,384]{1,0:T(8,128)(2,1)S(1)}, u32[]{:S(2)}, u32[]{:S(2)}) collective-permute-start(bf16[192,384]{1,0:T(8,128)(2,1)S(1)} %dynamic-slice_convert_fusion.3), channel_id=1, source_target_pairs={{0,8},{4,12},{8,0},{12,4},{16,24},{20,28},{24,16},{28,20},{1,9},{5... | collective-permute-start | bytes 442376 | tf_op jit(solution)/shard_map/ppermute | solution.py:699
  364.2 31.9 %copy-start.11 = (f32[4,56,384]{2,1,0:T(8,128)S(1)}, f32[4,56,384]{2,1,0:T(8,128)}, u32[]{:S(2)}) copy-start(f32[4,56,384]{2,1,0:T(8,128)} %constant_dynamic-slice_fusion) | copy-start | bytes 1032196
  367.9 7.2 %collective-permute-start.55 = (bf16[96,384]{1,0:T(8,128)(2,1)S(1)}, bf16[96,384]{1,0:T(8,128)(2,1)S(1)}, u32[]{:S(2)}, u32[]{:S(2)}) collective-permute-start(bf16[96,384]{1,0:T(8,128)(2,1)S(1)} %dynamic-slice_convert_fusion.6), channel_id=1, source_target_pairs={{0,16},{4,20},{8,24},{12,28},{16,0},{20,4},{24,8},{28,12},{1,17},{... | collective-permute-start | bytes 221192 | tf_op jit(solution)/shard_map/ppermute | solution.py:699
  375.1 5.4 %collective-permute-start.47 = (bf16[96,384]{1,0:T(8,128)(2,1)S(1)}, bf16[96,384]{1,0:T(8,128)(2,1)S(1)}, u32[]{:S(2)}, u32[]{:S(2)}) collective-permute-start(bf16[96,384]{1,0:T(8,128)(2,1)S(1)} %dynamic-slice_convert_fusion.7), channel_id=1, source_target_pairs={{0,16},{4,20},{8,24},{12,28},{16,0},{20,4},{24,8},{28,12},{1,17},{... | collective-permute-start | bytes 221192 | tf_op jit(solution)/shard_map/ppermute | solution.py:699
  380.5 5.3 %collective-permute-start.56 = (bf16[96,384]{1,0:T(8,128)(2,1)S(1)}, bf16[96,384]{1,0:T(8,128)(2,1)S(1)}, u32[]{:S(2)}, u32[]{:S(2)}) collective-permute-start(bf16[96,384]{1,0:T(8,128)(2,1)S(1)} %add_convert_fusion), channel_id=1, source_target_pairs={{0,16},{4,20},{8,24},{12,28},{16,0},{20,4},{24,8},{28,12},{1,17},{... | collective-permute-start | bytes 221192 | tf_op jit(solution)/shard_map/ppermute | solution.py:699
  385.7 5.3 %collective-permute-start.48 = (bf16[96,384]{1,0:T(8,128)(2,1)S(1)}, bf16[96,384]{1,0:T(8,128)(2,1)S(1)}, u32[]{:S(2)}, u32[]{:S(2)}) collective-permute-start(bf16[96,384]{1,0:T(8,128)(2,1)S(1)} %add_convert_fusion.1), channel_id=1, source_target_pairs={{0,16},{4,20},{8,24},{12,28},{16,0},{20,4},{24,8},{28,12},{1,17},{... | collective-permute-start | bytes 221192 | tf_op jit(solution)/shard_map/ppermute | solution.py:699
  391.0 5.1 %collective-permute-start.57 = (bf16[192,384]{1,0:T(8,128)(2,1)S(1)}, bf16[192,384]{1,0:T(8,128)(2,1)S(1)}, u32[]{:S(2)}, u32[]{:S(2)}) collective-permute-start(bf16[192,384]{1,0:T(8,128)(2,1)S(1)} %maximum_select_fusion.9), channel_id=1, source_target_pairs={{0,8},{4,12},{8,0},{12,4},{16,24},{20,28},{24,16},{28,20},{1,9},{5... | collective-permute-start | bytes 442376 | tf_op jit(solution)/shard_map/ppermute | solution.py:699
  393.0 5.2 %collective-permute-start.49 = (bf16[192,384]{1,0:T(8,128)(2,1)S(1)}, bf16[192,384]{1,0:T(8,128)(2,1)S(1)}, u32[]{:S(2)}, u32[]{:S(2)}) collective-permute-start(bf16[192,384]{1,0:T(8,128)(2,1)S(1)} %maximum_select_fusion.8), channel_id=1, source_target_pairs={{0,8},{4,12},{8,0},{12,4},{16,24},{20,28},{24,16},{28,20},{1,9},{5... | collective-permute-start | bytes 442376 | tf_op jit(solution)/shard_map/ppermute | solution.py:699
  396.1 9.5 %collective-permute-start.21 = (f32[4,56,384]{2,1,0:T(8,128)S(1)}, f32[4,56,384]{2,1,0:T(8,128)S(1)}, u32[]{:S(2)}, u32[]{:S(2)}) collective-permute-start(f32[4,56,384]{2,1,0:T(8,128)S(1)} %copy-done.11), channel_id=1, source_target_pairs={{1,2},{2,1},{5,6},{6,5},{9,10},{10,9},{13,14},{14,13},{17,18},{18,... | collective-permute-start | bytes 1032200 | tf_op jit(solution)/shard_map/ppermute | solution.py:695
  398.2 11.5 %collective-permute-start.58 = (bf16[384,384]{1,0:T(8,128)(2,1)S(1)}, bf16[384,384]{1,0:T(8,128)(2,1)S(1)}, u32[]{:S(2)}, u32[]{:S(2)}) collective-permute-start(bf16[384,384]{1,0:T(8,128)(2,1)S(1)} %maximum_select_fusion.5), channel_id=1, source_target_pairs={{0,4},{4,0},{8,12},{12,8},{16,20},{20,16},{24,28},{28,24},{1,5},{5... | collective-permute-start | bytes 884744 | tf_op jit(solution)/shard_map/ppermute | solution.py:699
  399.5 12.4 %collective-permute-start.50 = (bf16[384,384]{1,0:T(8,128)(2,1)S(1)}, bf16[384,384]{1,0:T(8,128)(2,1)S(1)}, u32[]{:S(2)}, u32[]{:S(2)}) collective-permute-start(bf16[384,384]{1,0:T(8,128)(2,1)S(1)} %maximum_select_fusion.4), channel_id=1, source_target_pairs={{0,4},{4,0},{8,12},{12,8},{16,20},{20,16},{24,28},{28,24},{1,5},{5... | collective-permute-start | bytes 884744 | tf_op jit(solution)/shard_map/ppermute | solution.py:699
  (36 other events, 149.6 us)
